TPU v7x, 512 devices: a whole 4x8x8 slice. The times are simulated.
512 devices in a mesh: freq: 8 (over y_hi, core), row: 64 (over z, y_lo, x).
Axes of the slice: x: 4, y: 8 (y_hi: 4, y_lo: 2; y = y_hi * 2 + y_lo), z: 8, core: 2. Of those that a mesh axis runs over, the one named last changes fastest.
Arguments:
- field: float32 [2, 8, 2048, 2048], P(None, 'freq', 'row'), may hold values from -6 to 6
- layer_index: int32 [2048], replicated, may hold values from 0 to 15
- layer_slowness: float32 [16], replicated, may hold values from 0.2223 to 0.6666
Outputs:
- sunk_field: float32 [2, 8, 2048, 2048], P(None, 'freq', None, 'row')
- image: float32 [128, 2048], P(None, 'row')
All inputs are finite; a program needn't handle non-finite values.
Results may differ from a plain program's by a relative error of at most 0.000078.
Values sent between devices are 32-bit elements; how exact they have to be, the bound alone decides.
No kernel may reach another device: no remote copies, remote signals or barrier semaphores. Data moves between devices by JAX's collectives and lax.ppermute only.
A program may use at most 64 MiB of HBM per device.

v0:
```python
import math

import jax
import jax.numpy as jnp
from jax import lax
from jax.sharding import PartitionSpec as P

HOFF = 128


depth_step = 0.0125
grid_step = 0.0125
slow_slow = 1.0 / 1.5
slow_fast = 1.0 / 4.5
highest = lax.Precision.HIGHEST


def cmul_stack(left, right):
    return jnp.stack(
        [left[0] * right[0] - left[1] * right[1], left[0] * right[1] + left[1] * right[0]]
    )


def block_matrix(angles):
    cosine = jnp.cos(angles)
    sine = jnp.sin(angles)
    return jnp.stack([jnp.stack([cosine, -sine]), jnp.stack([sine, cosine])])


def dft_tables(count, sign):
    first = 64
    second = count // first
    left = jnp.arange(first, dtype=jnp.int32)
    right = jnp.arange(second, dtype=jnp.int32)
    ang_one = (left[:, None] * left[None, :] % first).astype(jnp.float32) * (
        sign * 2.0 * math.pi / first
    )
    ang_two = (right[:, None] * right[None, :] % second).astype(jnp.float32) * (
        sign * 2.0 * math.pi / second
    )
    ang_tw = (left[:, None] * right[None, :]).astype(jnp.float32) * (sign * 2.0 * math.pi / count)
    return (
        block_matrix(ang_one),
        jnp.stack([jnp.cos(ang_tw), jnp.sin(ang_tw)]),
        block_matrix(ang_two),
    )


def transform_last(values, sign):
    count = values.shape[-1]
    mat_one, twiddle, mat_two = dft_tables(count, sign)
    lead = values.shape[:-1]
    split = values.reshape(lead + (64, count // 64))
    section = jnp.einsum("cdkn,d...nm->c...km", mat_one, split, precision=highest)
    section = cmul_stack(section, twiddle)
    section = jnp.einsum("d...kn,cdnl->c...lk", section, mat_two, precision=highest)
    return section.reshape(lead + (count,))


def transform_rows(values, sign):
    count = values.shape[-2]
    width = values.shape[-1]
    mat_one, twiddle, mat_two = dft_tables(count, sign)
    lead = values.shape[:-2]
    split = values.reshape(lead + (64, count // 64, width))
    section = jnp.einsum("cdkn,d...nqm->c...kqm", mat_one, split, precision=highest)
    section = cmul_stack(section, twiddle[:, :, :, None])
    section = jnp.einsum("d...kqm,cdql->c...lkm", section, mat_two, precision=highest)
    return section.reshape(lead + (count, width))


def wavenumbers(count):
    index = jnp.arange(count, dtype=jnp.int32)
    signed = jnp.where(index < count // 2, index, index - count)
    return signed.astype(jnp.float32) * (2.0 * math.pi / (count * grid_step))


def on_device(field, layer_index, layer_slowness):
    fcount = field.shape[1]
    count = field.shape[3]
    groups = lax.axis_size("row")
    block = count // groups
    total = fcount * lax.axis_size("freq")
    fidx = (lax.axis_index("freq") * fcount + jnp.arange(fcount, dtype=jnp.int32)).astype(
        jnp.float32
    )
    omegas = 2.0 * math.pi * (5.0 + 30.0 * (fidx + 0.5) / total)
    onehot = (
        layer_index[None, :] == jnp.arange(layer_slowness.shape[0], dtype=jnp.int32)[:, None]
    ).astype(jnp.float32)
    slowness = jnp.sum(layer_slowness[:, None] * onehot, axis=0)
    upper = (slow_slow - slowness) / (slow_slow - slow_fast)
    weights = (1.0 - upper, upper)
    refs = (slow_slow, slow_fast)
    knum = wavenumbers(count)
    prop_re, prop_im, corr_re, corr_im = ([], [], [], [])
    for j in range(2):
        quad = (omegas[:, None] * refs[j]) ** 2 - knum[None, :] ** 2
        mag = jnp.exp(-depth_step * jnp.sqrt(jnp.maximum(-quad, 0.0)))
        phase = -depth_step * jnp.sqrt(jnp.maximum(quad, 0.0))
        prop_re.append(mag * jnp.cos(phase))
        prop_im.append(mag * jnp.sin(phase))
        angle = -omegas[:, None] * depth_step * (slowness[None, :] - refs[j])
        corr_re.append(weights[j][None, :] * jnp.cos(angle) / count)
        corr_im.append(weights[j][None, :] * jnp.sin(angle) / count)
    props = jnp.stack([jnp.stack(prop_re), jnp.stack(prop_im)])
    corrs = jnp.stack([jnp.stack(corr_re), jnp.stack(corr_im)])
    spec = transform_last(field, -1.0)
    shifted = cmul_stack(spec[:, None], props[:, :, :, None, :])
    back = transform_last(shifted, 1.0)
    sunk = jnp.sum(cmul_stack(back, corrs[:, :, :, None, :]), axis=1)
    arrived = lax.all_to_all(sunk, "row", split_axis=3, concat_axis=2, tiled=True)
    col_spec = transform_rows(arrived, -1.0)
    moved = cmul_stack(col_spec[:, None], props[:, :, :, :, None])
    returned = transform_rows(moved, 1.0)
    sunk_field = jnp.sum(cmul_stack(returned, corrs[:, :, :, :, None]), axis=1)
    columns = lax.axis_index("row") * block + jnp.arange(block, dtype=jnp.int32)
    shot_at = (columns[None, :] + jnp.arange(HOFF, dtype=jnp.int32)[:, None] - HOFF // 2) % count
    picked = jnp.take_along_axis(sunk_field[0], shot_at[None], axis=1)
    terms = jnp.sum(picked, axis=0)
    image = lax.psum(terms, "freq")
    return (sunk_field, image)


def solution(mesh):
    return jax.shard_map(
        on_device,
        mesh=mesh,
        in_specs=(P(None, "freq", "row", None), P(), P()),
        out_specs=(P(None, "freq", None, "row"), P(None, "row")),
        check_vma=False,
    )
```

profile of v0, /device:TPU:8, one launch (start us, length us, event | category | flops | bytes accessed | tf_op | source)
XLA Modules:
  0.0 134.9 jit_solution(15099857533412500427)
XLA Ops:
  0.6 0.1 multiply_sine_fusion.1
  0.8 0.1 fusion.54
  1.2 0.1 multiply_sine_fusion
  1.4 0.1 fusion.55
  1.8 1.8 %reshape.1143 = f32[2,32,64,32]{3,2,1,0:T(8,128)S(1)} reshape(f32[2,1,32,2048]{3,2,1,0:T(8,128)} %param.3) | data formatting | bytes 1048576 | tf_op jit(solution)/shard_map/reshape.1
  3.6 3.4 %fusion.20 = f32[2,1,32,64,32]{3,4,2,0,1:T(8,128)S(1)} fusion(f32[2,32,64,32]{3,2,1,0:T(8,128)S(1)} %reshape.1143, f32[1,2,64,64]{3,2,1,0:T(8,128)S(1)} %get-tuple-element.37, f32[1,2,64,64]{3,2,1,0:T(8,128)S(1)} %get-tuple-element.36), kind=kOutput, calls=%fused_computation.23 | convolution fusion | flops 201342976 | bytes 1114112 | tf_op jit(solution)/shard_map/cdkn,d...nm->c...km/dot_general | solution.py:54
  7.1 0.2 multiply_subtract_fusion.7
  7.3 1.1 convolution_bitcast_fusion.2
  8.5 0.2 mul.1309
  8.7 0.3 copy.51
  9.0 0.2 mul.1321
  9.2 0.3 copy.52
  9.8 0.3 multiply_subtract_fusion.3
  10.1 1.9 %fusion.19 = f32[2,2,1,32,64,32]{4,5,0,3,1,2:T(8,128)S(1)} fusion(f32[1,2,1,32,64,32]{4,5,0,3,1,2:T(8,128)S(1)} %get-tuple-element.21, f32[1,2,1,32,64,32]{4,5,0,3,1,2:T(8,128)S(1)} %get-tuple-element.20, f32[1,2,64,64]{3,2,1,0:T(8,128)S(1)} %get-tuple-element.35, f32[1,2,64,64]{3,2,1,0:T(8,128)S(1)} %get-tuple-element.34), kind=kOutput, calls=%fused_computation.22 | convolution fusion | flops 402931712 | bytes 2162688 | tf_op jit(solution)/shard_map/cdkn,d...nm->c...km/dot_general | solution.py:54
  12.1 0.4 multiply_subtract_fusion.2
  12.5 0.6 copy-done.9
  13.1 2.1 %fusion.18 = f32[2,2,1,32,32,64]{5,4,3,1,0,2:T(8,128)S(1)} fusion(f32[1,2,1,32,64,32]{4,5,0,3,1,2:T(8,128)S(1)} %get-tuple-element.13, f32[1,2,1,32,64,32]{4,5,0,3,1,2:T(8,128)S(1)} %get-tuple-element.12, f32[1,2,32,32]{2,3,1,0:T(8,128)S(1)} %get-tuple-element.39, f32[1,2,32,32]{2,3,1,0:T(8,128)S(1)} %get-tuple-element.38), kind=kOutput, calls=%fused_computation.21 | convolution fusion | flops 201592832 | bytes 2113536 | tf_op jit(solution)/shard_map/d...kn,cdnl->c...lk/dot_general | solution.py:56
  15.2 0.2 fusion.67
  15.4 0.4 squeeze.8
  15.8 0.4 squeeze.9
  16.6 1.2 copy.53
  17.9 2.8 %reshape.1204 = f32[64,1,2048]{2,1,0:T(1,128)} reshape(f32[2048,1,2,32]{3,2,1,0:T(2,128)S(1)} %bitcast.201) | data formatting | bytes 1048576
  20.7 14.8 %all-to-all-start = ((f32[64,1,2048]{2,1,0:T(1,128)}), f32[64,1,2048]{2,1,0:T(1,128)S(1)}, u32[]{:S(2)}, u32[]{:S(2)}) async-start(f32[64,1,2048]{2,1,0:T(1,128)} %reshape.1204), calls=%async_computation | async-start | bytes 1048576 | tf_op jit(solution)/shard_map/all_to_all | solution.py:112
  35.7 17.9 %all-to-all-done = f32[64,1,2048]{2,1,0:T(1,128)S(1)} async-done(((f32[64,1,2048]{2,1,0:T(1,128)}), f32[64,1,2048]{2,1,0:T(1,128)S(1)}, u32[]{:S(2)}, u32[]{:S(2)}) %all-to-all-start) | async-done | bytes 524320 | tf_op jit(solution)/shard_map/all_to_all | solution.py:112
  53.6 0.5 broadcast.1556
  54.1 1.9 %reduce.2 = f32[64,2048]{1,0:T(8,128)S(1)} reduce(f32[64,1,2048]{2,1,0:T(1,128)S(1)} %all-to-all-done, f32[]{:T(128)} %broadcast.1556), dimensions={1}, to_apply=%all_to_all.11.reduce_sub_computation | reduce | bytes 1048580 | tf_op jit(solution)/shard_map/all_to_all | solution.py:112
  56.0 1.8 %reshape.1205 = f32[2048,1,2,32]{3,2,1,0:T(2,128)S(1)} reshape(f32[64,2048]{1,0:T(8,128)S(1)} %reduce.2) | data formatting | bytes 1048576
  57.8 1.4 %copy.55 = f32[2,1,32,64,32]{3,4,0,2,1:T(8,128)S(1)} copy(f32[2,1,32,64,32]{2,0,4,3,1:T(2,128)S(1)} %bitcast.202) | data formatting | bytes 1048576 | tf_op jit(solution)/shard_map/all_to_all | solution.py:112
  59.2 1.0 convolution_bitcast_fusion.1
  60.3 0.2 multiply_subtract_fusion.5
  60.6 0.4 copy-done.6
  61.0 1.6 %convolution_bitcast_fusion = f32[2,32,64,32]{2,1,3,0:T(8,128)S(1)} fusion(f32[2,64,32,32]{1,3,0,2:T(8,128)S(1)} %maximum_bitcast_fusion.14, f32[1,2,32,32]{2,3,1,0:T(8,128)S(1)} %copy-done.8, f32[1,2,32,32]{2,3,1,0:T(8,128)S(1)} %copy-done.6), kind=kOutput, calls=%fused_computation.24 | convolution fusion | flops 100667392 | bytes 1064960 | tf_op jit(solution)/shard_map/d...kqm,cdql->c...lkm/dot_general | solution.py:68
  62.7 0.2 mul.1365
  63.0 0.5 copy.57
  63.4 0.2 mul.1369
  63.7 0.5 copy.58
  64.2 0.3 multiply_subtract_fusion.1
  64.5 1.9 %fusion.17 = f32[2,2,1,64,32,32]{3,5,0,4,1,2:T(8,128)S(1)} fusion(f32[1,2,1,64,32,32]{3,5,0,4,1,2:T(8,128)S(1)} %get-tuple-element.19, f32[1,2,1,64,32,32]{3,5,0,4,1,2:T(8,128)S(1)} %get-tuple-element.18, f32[1,2,64,64]{3,2,1,0:T(8,128)S(1)} %get-tuple-element.35, f32[1,2,64,64]{3,2,1,0:T(8,128)S(1)} %get-tuple-element.34), kind=kOutput, calls=%fused_computation.20 | convolution fusion | flops 402931712 | bytes 2162688 | tf_op jit(solution)/shard_map/cdkn,d...nqm->c...kqm/dot_general | solution.py:66
  66.5 0.4 multiply_subtract_fusion
  66.9 0.3 maximum_bitcast_fusion.6
  67.2 0.4 copy-done.10
  67.6 3.1 %fusion.14 = f32[2,2,1,32,64,32]{4,3,5,1,0,2:T(8,128)S(1)} fusion(f32[2,2,64,32,32]{2,4,0,3,1:T(8,128)S(1)} %maximum_bitcast_fusion.6, f32[1,2,32,32]{2,3,1,0:T(8,128)S(1)} %copy-done.12, f32[1,2,32,32]{2,3,1,0:T(8,128)S(1)} %copy-done.10), kind=kOutput, calls=%fused_computation.19 | convolution fusion | flops 201330688 | bytes 2113536 | tf_op jit(solution)/shard_map/d...kqm,cdql->c...lkm/dot_general | solution.py:68
  70.7 0.2 fusion.66
  70.9 0.4 squeeze.10
  71.2 0.4 squeeze.11
  71.9 32.8 %gather_fusion = f32[4096]{0:T(1024)S(1)} fusion(f32[2048,32]{0,1:T(8,128)S(1)} %slice_bitcast_fusion, s32[4096]{0:T(1024)S(1)} %reshape.1176), kind=kCustom, calls=%fused_computation | custom fusion | bytes 65536 | tf_op jit(solution)/shard_map/jit(take_along_axis)/gather | solution.py:119
  104.8 29.4 %psum.7 = f32[128,32]{1,0:T(8,128)S(1)} all-reduce(f32[128,32]{1,0:T(8,128)S(1)} %and_select_fusion), channel_id=1, replica_groups=mesh['freq'=8,'row'=64] {'freq'}, use_global_device_ids=true, to_apply=%region_3.4 | all-reduce | flops 4096 | bytes 32768 | tf_op jit(solution)/shard_map/psum | solution.py:121
  134.2 0.7 copy.61
  (93 shorter events, 2.1 us)
Async XLA Ops:
  1.0 6.1 %copy-start.21 = (f32[64,32]{0,1:T(8,128)}, f32[64,32]{0,1:T(8,128)S(1)}, u32[]{:S(2)}) copy-start(f32[64,32]{0,1:T(8,128)S(1)} %get-tuple-element.52) | copy-start | bytes 24580
  1.0 6.1 %copy-start.23 = (f32[64,32]{0,1:T(8,128)}, f32[64,32]{0,1:T(8,128)S(1)}, u32[]{:S(2)}) copy-start(f32[64,32]{0,1:T(8,128)S(1)} %get-tuple-element.53) | copy-start | bytes 24580
  1.6 10.5 %copy-start.17 = (f32[64,32]{0,1:T(8,128)}, f32[64,32]{0,1:T(8,128)S(1)}, u32[]{:S(2)}) copy-start(f32[64,32]{0,1:T(8,128)S(1)} %get-tuple-element.58) | copy-start | bytes 24580
  1.6 10.5 %copy-start.19 = (f32[64,32]{0,1:T(8,128)}, f32[64,32]{0,1:T(8,128)S(1)}, u32[]{:S(2)}) copy-start(f32[64,32]{0,1:T(8,128)S(1)} %get-tuple-element.59) | copy-start | bytes 24580
  3.6 3.4 %copy-start.1 = (f32[1,2,64,64]{3,2,1,0:T(8,128)}, f32[1,2,64,64]{3,2,1,0:T(8,128)S(1)}, u32[]{:S(2)}) copy-start(f32[1,2,64,64]{3,2,1,0:T(8,128)S(1)} %get-tuple-element.36) | copy-start | bytes 98308
  3.6 3.4 %copy-start.3 = (f32[1,2,64,64]{3,2,1,0:T(8,128)}, f32[1,2,64,64]{3,2,1,0:T(8,128)S(1)}, u32[]{:S(2)}) copy-start(f32[1,2,64,64]{3,2,1,0:T(8,128)S(1)} %get-tuple-element.37) | copy-start | bytes 98308
  7.3 1.2 copy-start.5
  7.3 1.2 copy-start.7
  9.8 2.3 %copy-start.13 = (f32[2,64,32]{1,2,0:T(8,128)}, f32[2,64,32]{1,2,0:T(8,128)S(1)}, u32[]{:S(2)}) copy-start(f32[2,64,32]{1,2,0:T(8,128)S(1)} %pad_maximum_fusion.3) | copy-start | bytes 49156
  9.8 2.3 %copy-start.15 = (f32[2,64,32]{1,2,0:T(8,128)}, f32[2,64,32]{1,2,0:T(8,128)S(1)}, u32[]{:S(2)}) copy-start(f32[2,64,32]{1,2,0:T(8,128)S(1)} %pad_maximum_fusion.4) | copy-start | bytes 49156
  12.5 0.6 copy-start.9
  12.5 0.6 copy-start.11
  15.4 0.7 copy-start.29
  15.4 0.7 copy-start.32
  16.4 1.5 %copy-start.25 = (f32[2,2048]{1,0:T(2,128)}, f32[2,2048]{1,0:T(2,128)S(1)}, u32[]{:S(2)}) copy-start(f32[2,2048]{1,0:T(2,128)S(1)} %get-tuple-element.62) | copy-start | bytes 49156
  16.4 1.5 %copy-start.27 = (f32[2,2048]{1,0:T(2,128)}, f32[2,2048]{1,0:T(2,128)S(1)}, u32[]{:S(2)}) copy-start(f32[2,2048]{1,0:T(2,128)S(1)} %get-tuple-element.63) | copy-start | bytes 49156
  20.7 32.9 %all-to-all-start = ((f32[64,1,2048]{2,1,0:T(1,128)}), f32[64,1,2048]{2,1,0:T(1,128)S(1)}, u32[]{:S(2)}, u32[]{:S(2)}) async-start(f32[64,1,2048]{2,1,0:T(1,128)} %reshape.1204), calls=%async_computation | async-start | bytes 1048576 | tf_op jit(solution)/shard_map/all_to_all | solution.py:112
  35.5 20.5 %copy-start.30 = (s32[32]{0:T(128)}, s32[32]{0:T(128)S(1)}, u32[]{:S(2)}) copy-start(s32[32]{0:T(128)S(1)} %iota_add_fusion) | copy-start | bytes 388
  57.8 1.4 %copy-start.2 = (f32[1,2,64,64]{3,2,1,0:T(8,128)S(1)}, f32[1,2,64,64]{3,2,1,0:T(8,128)}, u32[]{:S(2)}) copy-start(f32[1,2,64,64]{3,2,1,0:T(8,128)} %copy-done.1) | copy-start | bytes 98308
  57.8 1.4 %copy-start.4 = (f32[1,2,64,64]{3,2,1,0:T(8,128)S(1)}, f32[1,2,64,64]{3,2,1,0:T(8,128)}, u32[]{:S(2)}) copy-start(f32[1,2,64,64]{3,2,1,0:T(8,128)} %copy-done.3) | copy-start | bytes 98308
  57.8 2.4 %copy-start.22 = (f32[64,32]{0,1:T(8,128)S(1)}, f32[64,32]{0,1:T(8,128)}, u32[]{:S(2)}) copy-start(f32[64,32]{0,1:T(8,128)} %copy-done.21) | copy-start | bytes 24580
  57.8 2.4 %copy-start.24 = (f32[64,32]{0,1:T(8,128)S(1)}, f32[64,32]{0,1:T(8,128)}, u32[]{:S(2)}) copy-start(f32[64,32]{0,1:T(8,128)} %copy-done.23) | copy-start | bytes 24580
  60.3 0.8 copy-start.6
  60.3 0.8 copy-start.8
  62.9 1.2 copy-start.14
  62.9 1.2 copy-start.16
  64.5 2.0 %copy-start.18 = (f32[64,32]{0,1:T(8,128)S(1)}, f32[64,32]{0,1:T(8,128)}, u32[]{:S(2)}) copy-start(f32[64,32]{0,1:T(8,128)} %copy-done.17) | copy-start | bytes 24580
  64.5 2.0 %copy-start.20 = (f32[64,32]{0,1:T(8,128)S(1)}, f32[64,32]{0,1:T(8,128)}, u32[]{:S(2)}) copy-start(f32[64,32]{0,1:T(8,128)} %copy-done.19) | copy-start | bytes 24580
  66.8 0.8 copy-start.10
  66.8 0.8 copy-start.12
  70.9 0.7 copy-start.26
  70.9 0.7 copy-start.28
  71.8 32.8 %copy-start = (f32[2,2048,32]{1,2,0:T(8,128)}, f32[2,2048,32]{1,2,0:T(8,128)S(1)}, u32[]{:S(2)}) copy-start(f32[2,2048,32]{1,2,0:T(8,128)S(1)} %maximum_reduce_fusion.1) | copy-start | bytes 1572868
  71.9 32.9 %copy-start.31 = (s32[32]{0:T(128)S(1)}, s32[32]{0:T(128)}, u32[]{:S(2)}) copy-start(s32[32]{0:T(128)} %copy-done.30) | copy-start | bytes 388
where the time goes:
time: 135 us
  local copies, waits for them, and re-layouts  49.1 us (36%)
  blocking collectives  29.4 us (22%)
  waiting for transfers between devices  17.9 us (13%)
  matrix products  16.1 us (12%)
  starting transfers between devices  14.8 us (11%)
  other arithmetic  6.02 us (4%)
  between operations  1.55 us (1%)
    gather x3, local copies, waits for them, and re-layouts, on_device(): picked = jnp.take_along_axis(sunk_field[0], shot_at[None], axis=1)  32.9 us
    psum x1, blocking collectives, on_device(): image = lax.psum(terms, 'freq')  29.4 us
    all_to_all x1, waiting for transfers between devices, on_device(): lax.all_to_all(sunk, 'row', split_axis=3, concat_axis=2, tiled=True)  17.9 us
    all_to_all x1, starting transfers between devices, on_device(): lax.all_to_all(sunk, 'row', split_axis=3, concat_axis=2, tiled=True)  14.8 us
    unnamed x69, local copies, waits for them, and re-layouts  6.9 us
    dot_general x2, matrix products, transform_last(): jnp.einsum('cdkn,d...nm->c...km', mat_one, split, precision=highest)  5.34 us
    dot_general x2, matrix products, transform_rows(): jnp.einsum('d...kqm,cdql->c...lkm', section, mat_two, precision=highest)  4.66 us
    dot_general x2, matrix products, transform_last(): jnp.einsum('d...kn,cdnl->c...lk', section, mat_two, precision=highest)  3.14 us
  transfers between devices with their start and end apart: 1, of which 1 were waited for; matrix products, arithmetic and copies ran while one was open for 0% of the time, Pallas kernels for 0%

commit v1 on v0

v1 whole, which is shorter than its diff:
```python
import math

import jax
import jax.numpy as jnp
import ml_dtypes
import numpy as np
from jax import lax
from jax.experimental import pallas as pl
from jax.experimental.pallas import tpu as pltpu
from jax.sharding import PartitionSpec as P

HOFF = 128
NX = 2048
NL = 16
BLOCK = 32
HIGH = 16
LANES = 128

depth_step = 0.0125
grid_step = 0.0125
slow_slow = 1.0 / 1.5
slow_fast = 1.0 / 4.5
refs = (slow_slow, slow_fast)


def split16(table):
    high = table.astype(np.float32).astype(ml_dtypes.bfloat16)
    low = (table - high.astype(np.float64)).astype(np.float32).astype(ml_dtypes.bfloat16)
    return high, low


def dft_weights():
    lane = np.arange(LANES)
    angle = 2.0 * math.pi * (lane[:, None] * lane[None, :] % LANES) / LANES
    cos, sin = np.cos(angle), np.sin(angle)
    forward = np.block([[cos, -sin], [sin, cos]])
    inverse = np.block([[cos, sin], [-sin, cos]])
    return np.stack(split16(forward) + split16(inverse))


def twiddle_table():
    angle = 2.0 * math.pi * np.arange(HIGH)[:, None] * np.arange(LANES)[None, :] / NX
    return np.stack([np.cos(angle), -np.sin(angle)]).astype(np.float32)


def omega_of(index, total):
    return 2.0 * math.pi * (5.0 + 30.0 * (index + 0.5) / total)


def propagators(total):
    index = np.arange(NX)
    knum = np.where(index < NX // 2, index, index - NX) * (2.0 * math.pi / (NX * grid_step))
    out = np.zeros((total, 2, 2, HIGH, LANES), np.float32)
    for f in range(total):
        for j in range(2):
            quad = (omega_of(f, total) * refs[j]) ** 2 - knum**2
            mag = np.exp(-depth_step * np.sqrt(np.maximum(-quad, 0.0)))
            phase = -depth_step * np.sqrt(np.maximum(quad, 0.0))
            out[f, j, 0] = (mag * np.cos(phase)).reshape(LANES, HIGH).T
            out[f, j, 1] = (mag * np.sin(phase)).reshape(LANES, HIGH).T
    return out


def add(a, b):
    return a[0] + b[0], a[1] + b[1]


def sub(a, b):
    return a[0] - b[0], a[1] - b[1]


def mul(a, b):
    return a[0] * b[0] - a[1] * b[1], a[0] * b[1] + a[1] * b[0]


def mul_conj(a, b):
    return a[0] * b[0] + a[1] * b[1], a[1] * b[0] - a[0] * b[1]


def fft4(x, sign):
    t0, t1 = add(x[0], x[2]), sub(x[0], x[2])
    t2, t3 = add(x[1], x[3]), sub(x[1], x[3])
    up = (t1[0] - t3[1], t1[1] + t3[0])
    down = (t1[0] + t3[1], t1[1] - t3[0])
    if sign < 0:
        up, down = down, up
    return [add(t0, t2), up, sub(t0, t2), down]


def turn(x, step, sign):
    step = step % 16
    if step == 0:
        return x
    if step == 4:
        return (x[1], -x[0]) if sign < 0 else (-x[1], x[0])
    root = math.sqrt(0.5)
    if step == 2:
        if sign < 0:
            return (x[0] + x[1]) * root, (x[1] - x[0]) * root
        return (x[0] - x[1]) * root, (x[1] + x[0]) * root
    angle = sign * 2.0 * math.pi * step / 16
    return mul(x, (math.cos(angle), math.sin(angle)))


def fft16(x, sign):
    parts = [fft4([x[4 * m + n] for m in range(4)], sign) for n in range(4)]
    out = [None] * 16
    for k in range(4):
        col = fft4([turn(parts[n][k], n * k, sign) for n in range(4)], sign)
        for m in range(4):
            out[k + 4 * m] = col[m]
    return out


def halves(x):
    high = x.astype(jnp.bfloat16)
    return high, (x - high.astype(jnp.float32)).astype(jnp.bfloat16)


def dot3(high, low, w_high, w_low):
    dot = lambda a, b: jnp.dot(a, b, preferred_element_type=jnp.float32)
    return dot(high, w_high) + dot(low, w_high) + dot(high, w_low)


def sink(x, w_ref, tw_ref, e_ref, corr):
    rows = x[0][0].shape[0]
    row = lambda ref, i: ref[pl.ds(i, 1), :]
    y = fft16(x, -1)
    y = [mul(y[k], (row(tw_ref.at[0], k), row(tw_ref.at[1], k))) for k in range(HIGH)]
    flat = jnp.concatenate([jnp.concatenate(v, axis=1) for v in y], axis=0)
    spec = dot3(*halves(flat), w_ref[0], w_ref[1])
    result = [None] * HIGH
    for j in range(2):
        moved = []
        for k in range(HIGH):
            part = spec[k * rows : (k + 1) * rows]
            e = (row(e_ref.at[0, j, 0], k), row(e_ref.at[0, j, 1], k))
            moved.append(jnp.concatenate(mul((part[:, :LANES], part[:, LANES:]), e), axis=1))
        back = dot3(*halves(jnp.concatenate(moved, axis=0)), w_ref[2], w_ref[3])
        v = []
        for k in range(HIGH):
            part = back[k * rows : (k + 1) * rows]
            v.append(
                mul_conj(
                    (part[:, :LANES], part[:, LANES:]), (row(tw_ref.at[0], k), row(tw_ref.at[1], k))
                )
            )
        v = fft16(v, 1)
        for a in range(HIGH):
            term = mul(v[a], corr(j, a))
            result[a] = term if j == 0 else add(result[a], term)
    return result


def fill_corrections(index_ref, slow_ref, omega, corr_ref):
    index = index_ref[...]
    slowness = jnp.zeros(index.shape, jnp.float32)
    for layer in range(NL):
        slowness = jnp.where(index == layer, slow_ref[layer], slowness)
    upper = (slow_slow - slowness) / (slow_slow - slow_fast)
    weights = (1.0 - upper, upper)
    for j in range(2):
        angle = -omega * depth_step * (slowness - refs[j])
        corr_ref[j, 0] = weights[j] * jnp.cos(angle) * (1.0 / NX)
        corr_ref[j, 1] = weights[j] * jnp.sin(angle) * (1.0 / NX)


def corr_rows(corr_ref):
    def get(j, a):
        return corr_ref[j, 0, pl.ds(a, 1), :], corr_ref[j, 1, pl.ds(a, 1), :]

    return get


def first_kernel(total, freq_ref, slow_ref, field_ref, index_ref, w_ref, tw_ref, e_ref, out_ref, corr_ref, sunk):
    omega = 2.0 * math.pi * (5.0 + 30.0 * (freq_ref[0].astype(jnp.float32) + 0.5) / total)
    fill_corrections(index_ref, slow_ref, omega, corr_ref)

    def rows16(h, _):
        at = pl.ds(pl.multiple_of(h * 16, 16), 16)
        x = [
            (field_ref[0, at, LANES * a : LANES * (a + 1)], field_ref[1, at, LANES * a : LANES * (a + 1)])
            for a in range(HIGH)
        ]
        u = sink(x, w_ref, tw_ref, e_ref, corr_rows(corr_ref))
        for a in range(HIGH):
            for c in range(2):
                base = (a % 2) * 64 + c * 32
                sunk[a // 2, pl.ds(pl.multiple_of(base + h * 16, 16), 16), :] = u[a][c]
        return 0

    lax.fori_loop(0, 2, rows16, 0)
    left = lax.broadcasted_iota(jnp.int32, (16, LANES), 1) < 64

    def pair(p, _):
        turned = sunk[p].T
        for q in range(4):
            upper = turned[32 * q : 32 * q + 16]
            lower = turned[32 * q + 16 : 32 * q + 32]
            first = jnp.where(left, upper, pltpu.roll(lower, 64, 1))
            second = jnp.where(left, pltpu.roll(upper, 64, 1), lower)
            out_ref[pl.ds(pl.multiple_of(p * 128 + 16 * q, 16), 16), :] = first
            out_ref[pl.ds(pl.multiple_of(p * 128 + 64 + 16 * q, 16), 16), :] = second
        return 0

    lax.fori_loop(0, HIGH // 2, pair, 0)


def second_kernel(freq_ref, block_ref, in_ref, corr_ref, w_ref, tw_ref, e_ref, out_ref, image_ref, lined):
    lane = lax.broadcasted_iota(jnp.int32, (16, LANES), 1)
    left = lane < 64
    even = lane % 64 < 32

    def regroup(a, _):
        g = [in_ref[pl.ds(pl.multiple_of(a * 64 + 16 * q, 16), 16), :] for q in range(4)]

        def swap(x, y, mask, width):
            return (
                jnp.where(mask, x, pltpu.roll(y, width, 1)),
                jnp.where(mask, pltpu.roll(x, LANES - width, 1), y),
            )

        p0, p2 = swap(g[0], g[2], left, 64)
        p1, p3 = swap(g[1], g[3], left, 64)
        o0, o1 = swap(p0, p1, even, 32)
        o2, o3 = swap(p2, p3, even, 32)
        lined[0, 0, a] = o0
        lined[0, 1, a] = o1
        lined[1, 0, a] = o2
        lined[1, 1, a] = o3
        return 0

    lax.fori_loop(0, HIGH, regroup, 0)

    def rows16(h, _):
        x = [(lined[h, 0, a], lined[h, 1, a]) for a in range(HIGH)]
        u = sink(x, w_ref, tw_ref, e_ref, corr_rows(corr_ref))
        at = pl.ds(pl.multiple_of(h * 16, 16), 16)
        for a in range(HIGH):
            for c in range(2):
                out_ref[c, at, LANES * a : LANES * (a + 1)] = u[a][c]
        return 0

    lax.fori_loop(0, 2, rows16, 0)
    start = (block_ref[0] * BLOCK + NX - HOFF // 2) % NX
    tile = start // LANES
    offset = start % LANES
    one = out_ref[0, :, pl.ds(pl.multiple_of(tile * LANES, LANES), LANES)]
    two = out_ref[0, :, pl.ds(pl.multiple_of((tile + 1) % HIGH * LANES, LANES), LANES)]
    band = jnp.concatenate([one, two], axis=1)
    row = lax.broadcasted_iota(jnp.int32, (BLOCK, 2 * LANES), 0) + offset
    for bit in range(7):
        step = 1 << bit
        band = jnp.where((row // step) % 2 == 1, pltpu.roll(band, 2 * LANES - step, 1), band)
    image_ref[...] = band[:, :LANES]


def on_device(field, layer_index, layer_slowness):
    total = lax.axis_size("freq")
    groups = lax.axis_size("row")
    weights = jnp.asarray(dft_weights())
    twiddles = jnp.asarray(twiddle_table())
    props = jnp.asarray(propagators(total))
    freq = lax.axis_index("freq").astype(jnp.int32).reshape(1)
    row = lax.axis_index("row").astype(jnp.int32).reshape(1)
    whole = lambda *shape: pl.BlockSpec(shape, lambda i, *_: (0,) * len(shape))
    mine = pl.BlockSpec((1, 2, 2, HIGH, LANES), lambda i, f, *_: (f[0], 0, 0, 0, 0))
    tables = [whole(4, 256, 256), whole(2, HIGH, LANES), mine]
    chunks, corr = pl.pallas_call(
        lambda *a: first_kernel(total, *a),
        out_shape=(
            jax.ShapeDtypeStruct((16 * groups, LANES), jnp.float32),
            jax.ShapeDtypeStruct((2, 2, HIGH, LANES), jnp.float32),
        ),
        grid_spec=pltpu.PrefetchScalarGridSpec(
            num_scalar_prefetch=2,
            grid=(1,),
            in_specs=[whole(2, BLOCK, NX), whole(HIGH, LANES)] + tables,
            out_specs=(whole(16 * groups, LANES), whole(2, 2, HIGH, LANES)),
            scratch_shapes=[pltpu.VMEM((HIGH // 2, LANES, LANES), jnp.float32)],
        ),
        compiler_params=pltpu.CompilerParams(vmem_limit_bytes=32 * 2**20),
        name="receiver_side",
    )(
        freq,
        layer_slowness,
        field.reshape(2, BLOCK, NX),
        layer_index.reshape(HIGH, LANES),
        weights,
        twiddles,
        props,
    )
    arrived = lax.all_to_all(chunks.reshape(groups, 1, NX), "row", 0, 0, tiled=True)
    sunk, image = pl.pallas_call(
        second_kernel,
        out_shape=(
            jax.ShapeDtypeStruct((2, BLOCK, NX), jnp.float32),
            jax.ShapeDtypeStruct((BLOCK, HOFF), jnp.float32),
        ),
        grid_spec=pltpu.PrefetchScalarGridSpec(
            num_scalar_prefetch=2,
            grid=(1,),
            in_specs=[whole(16 * groups, LANES), whole(2, 2, HIGH, LANES)] + tables,
            out_specs=(whole(2, BLOCK, NX), whole(BLOCK, HOFF)),
            scratch_shapes=[pltpu.VMEM((2, 2, HIGH, 16, LANES), jnp.float32)],
        ),
        compiler_params=pltpu.CompilerParams(vmem_limit_bytes=32 * 2**20),
        name="shot_side",
    )(freq, row, arrived.reshape(16 * groups, LANES), corr, weights, twiddles, props)
    image = jnp.swapaxes(lax.psum(image, "freq"), 0, 1)
    return jnp.swapaxes(sunk, 1, 2)[:, None], image


def solution(mesh):
    return jax.shard_map(
        on_device,
        mesh=mesh,
        in_specs=(P(None, "freq", "row", None), P(), P()),
        out_specs=(P(None, "freq", None, "row"), P(None, "row")),
        check_vma=False,
    )
```

time: 135 us -> 77.1 us (0.57)
  local copies, waits for them, and re-layouts: 49.1 us -> 4.44 us
  matrix products: 16.1 us -> 0 us
  Pallas kernels: 0 us -> 9 us
  other arithmetic: 6.02 us -> 0 us
    gather x3 -> x0, local copies, waits for them, and re-layouts: 32.9 us -> none  [on_device(): picked = jnp.take_along_axis(sunk_field[0], shot_at[None], axis=1)]
    dot_general x8 -> x0, matrix products: 16.1 us -> none  [the longest x2 5.34 us: transform_last(): jnp.einsum('cdkn,d...nm->c...km', mat_one, split, precision=highest)]
    pallas_call x0 -> x2, Pallas kernels: none -> 9 us  [the longest x1 4.69 us: on_device(): pl.pallas_call(second_kernel, out_shape=(jax.ShapeDtypeStruct((2, BLOCK,...]
    unnamed x69 -> x16, local copies, waits for them, and re-layouts: 6.9 us -> 4.44 us
    mul x8 -> x0, local copies, waits for them, and re-layouts: 2.44 us -> none  [the longest x4 1.23 us: cmul_stack(): left[1] * right[1]]
    sub x8 -> x0, other arithmetic: 1.93 us -> none  [cmul_stack(): left[0] * right[0] - left[1] * right[1]]
    all_to_all x1 -> x0, other arithmetic: 1.88 us -> none  [on_device(): lax.all_to_all(sunk, 'row', split_axis=3, concat_axis=2, tiled=True)]
    all_to_all x2 -> x0, local copies, waits for them, and re-layouts: 1.88 us -> none  [on_device(): lax.all_to_all(sunk, 'row', split_axis=3, concat_axis=2, tiled=True)]
where the time goes in v1:
time: 77.1 us; the launch traced here: 76.7 us
  blocking collectives  29.6 us (38%)
  waiting for transfers between devices  18.1 us (23%)
  starting transfers between devices  14.9 us (19%)
  Pallas kernels  9 us (12%)
  local copies, waits for them, and re-layouts  4.44 us (6%)
    psum x1, blocking collectives, on_device(): image = jnp.swapaxes(lax.psum(image, 'freq'), 0, 1)  29.6 us
    all_to_all x1, waiting for transfers between devices, on_device(): lax.all_to_all(chunks.reshape(groups, 1, NX), 'row', 0, 0, tiled=True)  18.1 us
    all_to_all x1, starting transfers between devices, on_device(): lax.all_to_all(chunks.reshape(groups, 1, NX), 'row', 0, 0, tiled=True)  14.9 us
    pallas_call x1, Pallas kernels, on_device(): pl.pallas_call(second_kernel, out_shape=(jax.ShapeDtypeStruct((2, BLOCK,...  4.69 us
    unnamed x16, local copies, waits for them, and re-layouts  4.44 us
    pallas_call x1, Pallas kernels, on_device(): pl.pallas_call(lambda *a: first_kernel(total, *a), out_shape=(jax.ShapeDt...  4.31 us
  transfers between devices with their start and end apart: 1, of which 1 were waited for; matrix products, arithmetic and copies ran while one was open for 0% of the time, Pallas kernels for 0%

profile of v1, /device:TPU:8, one launch (start us, length us, event | category | flops | bytes accessed | tf_op | source)
XLA Modules:
  0.0 76.7 jit_solution(9623009256223301809)
XLA Ops:
  0.6 0.0 copy-start.5
  0.6 0.0 copy-start.7
  0.7 0.7 copy-done.5
  1.4 0.0 copy-done.7
  1.4 0.0 copy-start
  1.4 1.0 %copy-done = bf16[4,256,256]{2,1,0:T(8,128)(2,1)S(1)} copy-done((bf16[4,256,256]{2,1,0:T(8,128)(2,1)S(1)}, bf16[4,256,256]{2,1,0:T(8,128)(2,1)}, u32[]{:S(2)}) %copy-start) | copy-done | bytes 524312
  2.4 0.0 copy-start.2
  2.4 0.9 %copy-done.2 = f32[8,2,2,16,128]{4,3,2,1,0:T(8,128)S(1)} copy-done((f32[8,2,2,16,128]{4,3,2,1,0:T(8,128)S(1)}, f32[8,2,2,16,128]{4,3,2,1,0:T(8,128)}, u32[]{:S(2)}) %copy-start.2) | copy-done | bytes 262168
  3.3 0.0 copy-start.4
  3.3 1.0 %copy-done.4 = f32[2,1,32,2048]{3,2,1,0:T(8,128)S(1)} copy-done((f32[2,1,32,2048]{3,2,1,0:T(8,128)S(1)}, f32[2,1,32,2048]{3,2,1,0:T(8,128)}, u32[]{:S(2)}) %copy-start.4) | copy-done | bytes 524312
  4.4 0.0 copy-start.6
  4.4 0.7 copy-done.6
  5.1 4.3 %receiver_side.1 = (f32[1024,128]{1,0:T(8,128)}, f32[2,2,16,128]{3,2,1,0:T(8,128)S(1)}) custom-call(s32[1]{0:T(128)} %bitcast.a_0_.freq_ref, f32[16]{0:T(128)S(1)} %copy-done.7, f32[2,32,2048]{2,1,0:T(8,128)S(1)} %bitcast.13, s32[16,128]{1,0:T(8,128)S(1)} %bitcast.15, bf16[4,256,256]{2,1,0:T(8,128)(2,1)S(1)} %copy-done, f32[2,16,128]{2,1,0:T(8,128)S(1)} %copy-done.5, ...), custom_call_target="tpu_custom_call" | custom-call | tf_op jit(solution)/shard_map/receiver_side/pallas_call | solution.py:269
  9.4 0.0 copy-start.1
  9.4 0.0 copy-start.3
  9.4 14.9 %all-to-all-start = ((f32[64,1,2048]{2,1,0:T(1,128)}), f32[64,1,2048]{2,1,0:T(1,128)S(1)}, u32[]{:S(2)}, u32[]{:S(2)}) async-start(f32[64,1,2048]{2,1,0:T(1,128)} %bitcast.4), calls=%async_computation | async-start | bytes 1048576 | tf_op jit(solution)/shard_map/all_to_all | solution.py:293
  24.3 18.1 %all-to-all-done = f32[64,1,2048]{2,1,0:T(1,128)S(1)} async-done(((f32[64,1,2048]{2,1,0:T(1,128)}), f32[64,1,2048]{2,1,0:T(1,128)S(1)}, u32[]{:S(2)}, u32[]{:S(2)}) %all-to-all-start) | async-done | bytes 524320 | tf_op jit(solution)/shard_map/all_to_all | solution.py:293
  42.5 0.0 copy-done.1
  42.5 0.0 copy-done.3
  42.5 4.7 %shot_side.1 = (f32[2,32,2048]{2,1,0:T(8,128)}, f32[32,128]{1,0:T(8,128)S(1)}) custom-call(s32[1]{0:T(128)} %bitcast.a_0_.freq_ref, s32[1]{0:T(128)} %bitcast.1.block_ref, f32[1024,128]{1,0:T(8,128)S(1)} %bitcast.12, f32[2,2,16,128]{3,2,1,0:T(8,128)S(1)} %get-tuple-element.7.corr_ref, bf16[4,256,256]{2,1,0:T(8,128)(2,1)S(1)} %copy-done.1, ...), custom_call_target="tpu_custom_call" | custom-call | tf_op jit(solution)/shard_map/shot_side/pallas_call | solution.py:294
  47.1 29.6 %psum.7 = f32[128,32]{0,1:T(8,128)} all-reduce(f32[128,32]{0,1:T(8,128)S(1)} %bitcast.14), channel_id=1, replica_groups=mesh['freq'=8,'row'=64] {'freq'}, use_global_device_ids=true, to_apply=%region_0.0 | all-reduce | flops 4096 | bytes 32768 | tf_op jit(solution)/shard_map/psum | solution.py:310
Async XLA Ops:
  0.6 0.7 copy-start.5
  0.6 0.7 copy-start.7
  1.4 1.0 %copy-start = (bf16[4,256,256]{2,1,0:T(8,128)(2,1)S(1)}, bf16[4,256,256]{2,1,0:T(8,128)(2,1)}, u32[]{:S(2)}) copy-start(bf16[4,256,256]{2,1,0:T(8,128)(2,1)} %constant.15.clone.a_4_.w_ref) | copy-start | bytes 1572868
  2.4 0.9 %copy-start.2 = (f32[8,2,2,16,128]{4,3,2,1,0:T(8,128)S(1)}, f32[8,2,2,16,128]{4,3,2,1,0:T(8,128)}, u32[]{:S(2)}) copy-start(f32[8,2,2,16,128]{4,3,2,1,0:T(8,128)} %constant.17.clone.a_6_.e_ref) | copy-start | bytes 786436
  3.3 1.0 %copy-start.4 = (f32[2,1,32,2048]{3,2,1,0:T(8,128)S(1)}, f32[2,1,32,2048]{3,2,1,0:T(8,128)}, u32[]{:S(2)}) copy-start(f32[2,1,32,2048]{3,2,1,0:T(8,128)} %param.6) | copy-start | bytes 1572868
  4.4 0.7 copy-start.6
  9.4 33.1 %copy-start.1 = (bf16[4,256,256]{2,1,0:T(8,128)(2,1)S(1)}, bf16[4,256,256]{2,1,0:T(8,128)(2,1)}, u32[]{:S(2)}) copy-start(bf16[4,256,256]{2,1,0:T(8,128)(2,1)} %constant.15.clone.a_4_.w_ref) | copy-start | bytes 1572868
  9.4 33.1 %copy-start.3 = (f32[8,2,2,16,128]{4,3,2,1,0:T(8,128)S(1)}, f32[8,2,2,16,128]{4,3,2,1,0:T(8,128)}, u32[]{:S(2)}) copy-start(f32[8,2,2,16,128]{4,3,2,1,0:T(8,128)} %constant.17.clone.a_6_.e_ref) | copy-start | bytes 786436
  9.4 33.0 %all-to-all-start = ((f32[64,1,2048]{2,1,0:T(1,128)}), f32[64,1,2048]{2,1,0:T(1,128)S(1)}, u32[]{:S(2)}, u32[]{:S(2)}) async-start(f32[64,1,2048]{2,1,0:T(1,128)} %bitcast.4), calls=%async_computation | async-start | bytes 1048576 | tf_op jit(solution)/shard_map/all_to_all | solution.py:293

commit v2 on v1

v2 whole, which is shorter than its diff:
```python
import math

import jax
import jax.numpy as jnp
import ml_dtypes
import numpy as np
from jax import lax
from jax.experimental import pallas as pl
from jax.experimental.pallas import tpu as pltpu
from jax.sharding import PartitionSpec as P

HOFF = 128
NX = 2048
NL = 16
BLOCK = 32
HIGH = 16
LANES = 128

depth_step = 0.0125
grid_step = 0.0125
slow_slow = 1.0 / 1.5
slow_fast = 1.0 / 4.5
refs = (slow_slow, slow_fast)


def split16(table):
    high = table.astype(np.float32).astype(ml_dtypes.bfloat16)
    low = (table - high.astype(np.float64)).astype(np.float32).astype(ml_dtypes.bfloat16)
    return high, low


def dft_weights():
    lane = np.arange(LANES)
    angle = 2.0 * math.pi * (lane[:, None] * lane[None, :] % LANES) / LANES
    cos, sin = np.cos(angle), np.sin(angle)
    forward = np.block([[cos, -sin], [sin, cos]])
    inverse = np.block([[cos, sin], [-sin, cos]])
    return np.stack(split16(forward) + split16(inverse))


def twiddle_table():
    angle = 2.0 * math.pi * np.arange(HIGH)[:, None] * np.arange(LANES)[None, :] / NX
    return np.stack([np.cos(angle), -np.sin(angle)]).astype(np.float32)


def omega_of(index, total):
    return 2.0 * math.pi * (5.0 + 30.0 * (index + 0.5) / total)


def propagators(total):
    index = np.arange(NX)
    knum = np.where(index < NX // 2, index, index - NX) * (2.0 * math.pi / (NX * grid_step))
    out = np.zeros((total, 2, 2, HIGH, LANES), np.float32)
    for f in range(total):
        for j in range(2):
            quad = (omega_of(f, total) * refs[j]) ** 2 - knum**2
            mag = np.exp(-depth_step * np.sqrt(np.maximum(-quad, 0.0)))
            phase = -depth_step * np.sqrt(np.maximum(quad, 0.0))
            out[f, j, 0] = (mag * np.cos(phase)).reshape(LANES, HIGH).T
            out[f, j, 1] = (mag * np.sin(phase)).reshape(LANES, HIGH).T
    return out


def add(a, b):
    return a[0] + b[0], a[1] + b[1]


def sub(a, b):
    return a[0] - b[0], a[1] - b[1]


def mul(a, b):
    return a[0] * b[0] - a[1] * b[1], a[0] * b[1] + a[1] * b[0]


def mul_conj(a, b):
    return a[0] * b[0] + a[1] * b[1], a[1] * b[0] - a[0] * b[1]


def fft4(x, sign):
    t0, t1 = add(x[0], x[2]), sub(x[0], x[2])
    t2, t3 = add(x[1], x[3]), sub(x[1], x[3])
    up = (t1[0] - t3[1], t1[1] + t3[0])
    down = (t1[0] + t3[1], t1[1] - t3[0])
    if sign < 0:
        up, down = down, up
    return [add(t0, t2), up, sub(t0, t2), down]


def turn(x, step, sign):
    step = step % 16
    if step == 0:
        return x
    if step == 4:
        return (x[1], -x[0]) if sign < 0 else (-x[1], x[0])
    root = math.sqrt(0.5)
    if step == 2:
        if sign < 0:
            return (x[0] + x[1]) * root, (x[1] - x[0]) * root
        return (x[0] - x[1]) * root, (x[1] + x[0]) * root
    angle = sign * 2.0 * math.pi * step / 16
    return mul(x, (math.cos(angle), math.sin(angle)))


def fft16(x, sign):
    parts = [fft4([x[4 * m + n] for m in range(4)], sign) for n in range(4)]
    out = [None] * 16
    for k in range(4):
        col = fft4([turn(parts[n][k], n * k, sign) for n in range(4)], sign)
        for m in range(4):
            out[k + 4 * m] = col[m]
    return out


def halves(x):
    high = x.astype(jnp.bfloat16)
    return high, (x - high.astype(jnp.float32)).astype(jnp.bfloat16)


def dot3(high, low, w_high, w_low):
    dot = lambda a, b: jnp.dot(a, b, preferred_element_type=jnp.float32)
    return dot(high, w_high) + dot(low, w_high) + dot(high, w_low)


def row(ref, i):
    return ref[pl.ds(i, 1), :]


def spread(x, w_ref, tw_ref, e_ref):
    rows = x[0][0].shape[0]
    twiddle = lambda k: (row(tw_ref.at[0], k), row(tw_ref.at[1], k))
    y = fft16(x, -1)
    flat = jnp.concatenate(
        [jnp.concatenate(mul(y[k], twiddle(k)), axis=1) for k in range(HIGH)], axis=0
    )
    spec = dot3(*halves(flat), w_ref[0], w_ref[1])
    for j in range(2):
        moved = []
        for k in range(HIGH):
            part = spec[k * rows : (k + 1) * rows]
            e = (row(e_ref.at[0, j, 0], k), row(e_ref.at[0, j, 1], k))
            moved.append(jnp.concatenate(mul((part[:, :LANES], part[:, LANES:]), e), axis=1))
        back = dot3(*halves(jnp.concatenate(moved, axis=0)), w_ref[2], w_ref[3])
        tiles = []
        for k in range(HIGH):
            part = back[k * rows : (k + 1) * rows]
            tiles.append(mul_conj((part[:, :LANES], part[:, LANES:]), twiddle(k)))
        yield j, tiles


def corr_row(corr_ref, j, a):
    return row(corr_ref.at[j, 0], a), row(corr_ref.at[j, 1], a)


def gather_up(corr_ref, tiles_of):
    result = [None] * HIGH
    for j, tiles in tiles_of:
        v = fft16(tiles, 1)
        for a in range(HIGH):
            term = mul(v[a], corr_row(corr_ref, j, a))
            result[a] = term if j == 0 else add(result[a], term)
    return result


def fill_corrections(index_ref, slow_ref, omega, corr_ref):
    index = index_ref[...]
    slowness = jnp.zeros(index.shape, jnp.float32)
    for layer in range(NL):
        slowness = jnp.where(index == layer, slow_ref[layer], slowness)
    upper = (slow_slow - slowness) / (slow_slow - slow_fast)
    weights = (1.0 - upper, upper)
    for j in range(2):
        angle = -omega * depth_step * (slowness - refs[j])
        corr_ref[j, 0] = weights[j] * jnp.cos(angle) * (1.0 / NX)
        corr_ref[j, 1] = weights[j] * jnp.sin(angle) * (1.0 / NX)


def first_kernel(
    total, slow_hbm, index_hbm, field_hbm, tw_hbm, w_hbm, e_hbm, out_ref, corr_ref,
    slow_ref, index_ref, field_ref, tw_ref, w_ref, e_ref, sunk, sems,
):
    freq = lax.axis_index("freq")
    pairs = [
        (slow_hbm, slow_ref),
        (index_hbm, index_ref),
        (field_hbm, field_ref),
        (tw_hbm, tw_ref),
        (w_hbm, w_ref),
        (e_hbm.at[pl.ds(freq, 1)], e_ref),
    ]
    copies = [pltpu.make_async_copy(s, d, sems.at[i]) for i, (s, d) in enumerate(pairs)]
    for copy in copies:
        copy.start()
    copies[0].wait()
    copies[1].wait()
    omega = 2.0 * math.pi * (5.0 + 30.0 * (freq.astype(jnp.float32) + 0.5) / total)
    fill_corrections(index_ref, slow_ref, omega, corr_ref)
    for copy in copies[2:]:
        copy.wait()

    def rows16(h, _):
        at = pl.ds(pl.multiple_of(h * 16, 16), 16)
        x = [
            (field_ref[0, at, LANES * a : LANES * (a + 1)], field_ref[1, at, LANES * a : LANES * (a + 1)])
            for a in range(HIGH)
        ]
        u = gather_up(corr_ref, spread(x, w_ref, tw_ref, e_ref))
        for a in range(HIGH):
            for c in range(2):
                base = (a % 2) * 64 + c * 32
                sunk[a // 2, pl.ds(pl.multiple_of(base + h * 16, 16), 16), :] = u[a][c]
        return 0

    lax.fori_loop(0, 2, rows16, 0)
    left = lax.broadcasted_iota(jnp.int32, (16, LANES), 1) < 64
    for p in range(HIGH // 2):
        turned = sunk[p].T
        for q in range(4):
            upper = turned[32 * q : 32 * q + 16]
            lower = turned[32 * q + 16 : 32 * q + 32]
            first = jnp.where(left, upper, pltpu.roll(lower, 64, 1))
            second = jnp.where(left, pltpu.roll(upper, 64, 1), lower)
            out_ref[p * 128 + 16 * q : p * 128 + 16 * q + 16, :] = first
            out_ref[p * 128 + 64 + 16 * q : p * 128 + 80 + 16 * q, :] = second


def second_kernel(root_ref, in_ref, corr_ref, w_ref, tw_ref, e_all, parts_ref, image_hbm, lined, image_ref, sems):
    lane = lax.broadcasted_iota(jnp.int32, (16, LANES), 1)
    left = lane < 64
    even = (lane & 63) < 32
    e_ref = e_all.at[pl.ds(lax.axis_index("freq"), 1)]

    def swap(x, y, mask, width):
        return (
            jnp.where(mask, x, pltpu.roll(y, width, 1)),
            jnp.where(mask, pltpu.roll(x, LANES - width, 1), y),
        )

    for a in range(HIGH):
        g = [in_ref[a * 64 + 16 * q : a * 64 + 16 * q + 16, :] for q in range(4)]
        p0, p2 = swap(g[0], g[2], left, 64)
        p1, p3 = swap(g[1], g[3], left, 64)
        lined[0, 0, a], lined[0, 1, a] = swap(p0, p1, even, 32)
        lined[1, 0, a], lined[1, 1, a] = swap(p2, p3, even, 32)

    start = (lax.axis_index("row") * BLOCK + NX - HOFF // 2) & (NX - 1)
    tile = start // LANES
    offset = start & (LANES - 1)

    def rows16(h, _):
        x = [(lined[h, 0, a], lined[h, 1, a]) for a in range(HIGH)]
        at = pl.ds(pl.multiple_of(h * 16, 16), 16)
        band = [0.0, 0.0]
        for j, tiles in spread(x, w_ref, tw_ref, e_ref):
            for k in range(HIGH):
                parts_ref[j, 0, k, at, :] = tiles[k][0]
                parts_ref[j, 1, k, at, :] = tiles[k][1]
            for i in range(2):
                a = (tile + i) & (HIGH - 1)
                here = None
                for k in range(HIGH):
                    turned = mul(tiles[k], (root_ref[0, (a * k) & 15], root_ref[1, (a * k) & 15]))
                    here = turned if here is None else add(here, turned)
                c = corr_row(corr_ref, j, a)
                band[i] = band[i] + here[0] * c[0] - here[1] * c[1]
        image_ref[at, :] = jnp.concatenate(band, axis=1)
        return 0

    lax.fori_loop(0, 2, rows16, 0)
    band = image_ref[...]
    for width in (64, 32):
        band = jnp.where((offset & width) != 0, pltpu.roll(band, 2 * LANES - width, 1), band)
    line = lax.broadcasted_iota(jnp.int32, band.shape, 0)
    for width in (16, 8, 4, 2, 1):
        band = jnp.where((line & width) != 0, pltpu.roll(band, 2 * LANES - width, 1), band)
    image_ref[:, :LANES] = band[:, :LANES]
    copies = [
        pltpu.make_async_copy(image_ref.at[:, pl.ds(0, LANES)], image_hbm.at[f], sems.at[f])
        for f in range(image_hbm.shape[0])
    ]
    for copy in copies:
        copy.start()
    for copy in copies:
        copy.wait()


def third_kernel(parts_ref, corr_ref, out_ref):
    def rows16(h, _):
        at = pl.ds(pl.multiple_of(h * 16, 16), 16)
        tiles_of = [
            (j, [(parts_ref[j, 0, k, at, :], parts_ref[j, 1, k, at, :]) for k in range(HIGH)])
            for j in range(2)
        ]
        u = gather_up(corr_ref, tiles_of)
        for a in range(HIGH):
            for c in range(2):
                out_ref[c, at, LANES * a : LANES * (a + 1)] = u[a][c]
        return 0

    lax.fori_loop(0, 2, rows16, 0)


def on_device(field, layer_index, layer_slowness):
    total = lax.axis_size("freq")
    groups = lax.axis_size("row")
    weights = jnp.asarray(dft_weights())
    twiddles = jnp.asarray(twiddle_table())
    props = jnp.asarray(propagators(total))
    angle = 2.0 * math.pi * np.arange(16) / 16
    roots = jnp.asarray(np.stack([np.cos(angle), np.sin(angle)]).astype(np.float32))
    shape = lambda *dims: jax.ShapeDtypeStruct(dims, jnp.float32)
    keep = lambda *dims: pltpu.VMEM(dims, jnp.float32)
    vmem = pl.BlockSpec(memory_space=pltpu.VMEM)
    smem = pl.BlockSpec(memory_space=pltpu.SMEM)
    hbm = pl.BlockSpec(memory_space=pltpu.HBM)
    stay = lambda x: pltpu.with_memory_space_constraint(x, pltpu.HBM)
    near = lambda x: pltpu.with_memory_space_constraint(x, pltpu.VMEM)
    params = pltpu.CompilerParams(vmem_limit_bytes=32 * 2**20)
    cost = lambda n: pl.CostEstimate(flops=n, bytes_accessed=2**20, transcendentals=0)
    chunks, corr = pl.pallas_call(
        lambda *a: first_kernel(total, *a),
        out_shape=(keep(16 * groups, LANES), keep(2, 2, HIGH, LANES)),
        in_specs=[hbm] * 6,
        out_specs=(vmem, vmem),
        scratch_shapes=[
            pltpu.SMEM((NL,), jnp.float32),
            pltpu.VMEM((HIGH, LANES), jnp.int32),
            pltpu.VMEM((2, BLOCK, NX), jnp.float32),
            pltpu.VMEM((2, HIGH, LANES), jnp.float32),
            pltpu.VMEM((4, 256, 256), jnp.bfloat16),
            pltpu.VMEM((1, 2, 2, HIGH, LANES), jnp.float32),
            pltpu.VMEM((HIGH // 2, LANES, LANES), jnp.float32),
            pltpu.SemaphoreType.DMA((6,)),
        ],
        compiler_params=params,
        cost_estimate=cost(10**9),
        name="receiver_side",
    )(
        stay(layer_slowness),
        stay(layer_index.reshape(HIGH, LANES)),
        stay(field.reshape(2, BLOCK, NX)),
        stay(twiddles),
        stay(weights),
        stay(props),
    )
    arrived = lax.all_to_all(chunks.reshape(groups, 16, LANES), "row", 0, 0, tiled=True)
    parts, image = pl.pallas_call(
        second_kernel,
        out_shape=(keep(2, 2, HIGH, BLOCK, LANES), pltpu.HBM((total, BLOCK, HOFF), jnp.float32)),
        in_specs=[smem] + [vmem] * 5,
        out_specs=(vmem, hbm),
        scratch_shapes=[
            pltpu.VMEM((2, 2, HIGH, 16, LANES), jnp.float32),
            pltpu.VMEM((BLOCK, 2 * LANES), jnp.float32),
            pltpu.SemaphoreType.DMA((total,)),
        ],
        compiler_params=params,
        cost_estimate=cost(10**9),
        name="shot_side",
    )(roots, arrived.reshape(16 * groups, LANES), corr, weights, twiddles, props)
    images = lax.all_to_all(image, "freq", 0, 0, tiled=True)
    sunk = pl.pallas_call(
        third_kernel,
        out_shape=shape(2, BLOCK, NX),
        in_specs=[vmem, vmem],
        out_specs=vmem,
        compiler_params=params,
        cost_estimate=cost(10**8),
        name="shot_side_end",
    )(near(parts), near(corr))
    image = jnp.swapaxes(jnp.sum(images, axis=0), 0, 1)
    return jnp.swapaxes(sunk, 1, 2)[:, None], image


def solution(mesh):
    return jax.shard_map(
        on_device,
        mesh=mesh,
        in_specs=(P(None, "freq", "row", None), P(), P()),
        out_specs=(P(None, "freq", None, "row"), P(None, "row")),
        check_vma=False,
    )
```

time: 77.1 us -> 58.7 us (0.76)
  the two profiles are of different devices: /device:TPU:8 before, /device:TPU:1 now
where the time goes in v2:
time: 58.7 us; the launch traced here: 58.4 us
  blocking collectives  32.3 us (55%)
  starting transfers between devices  8.8 us (15%)
  Pallas kernels  8.57 us (15%)
  waiting for transfers between devices  6.83 us (12%)
  local copies, waits for them, and re-layouts  0.69 us (1%)
  between operations  0.68 us (1%)
  other arithmetic  0.62 us (1%)
    all_to_all x1, blocking collectives, on_device(): lax.all_to_all(chunks.reshape(groups, 16, LANES), 'row', 0, 0, tiled=True)  32.3 us
    all_to_all x1, starting transfers between devices, on_device(): images = lax.all_to_all(image, 'freq', 0, 0, tiled=True)  8.8 us
    all_to_all x1, waiting for transfers between devices, on_device(): images = lax.all_to_all(image, 'freq', 0, 0, tiled=True)  6.83 us
    pallas_call x1, Pallas kernels, on_device(): pl.pallas_call(second_kernel, out_shape=(keep(2, 2, HIGH, BLOCK, LANES),...  4.15 us
    pallas_call x1, Pallas kernels, on_device(): pl.pallas_call(lambda *a: first_kernel(total, *a), out_shape=(keep(16 * g...  3.22 us
    pallas_call x1, Pallas kernels, on_device(): pl.pallas_call(third_kernel, out_shape=shape(2, BLOCK, NX), in_specs=[vme...  1.2 us
  transfers between devices with their start and end apart: 1, of which 1 were waited for; matrix products, arithmetic and copies ran while one was open for 0% of the time, Pallas kernels for 2%

profile of v2, /device:TPU:1, one launch (start us, length us, event | category | flops | bytes accessed | tf_op | source)
XLA Modules:
  0.0 58.4 jit_solution(13263708311388900613)
XLA Ops:
  0.6 3.2 %receiver_side.1 = (f32[1024,128]{1,0:T(8,128)S(1)}, f32[2,2,16,128]{3,2,1,0:T(8,128)S(1)}) custom-call(f32[16]{0:T(128)} %a_0_.1, s32[16,128]{1,0:T(8,128)} %bitcast.15, f32[2,32,2048]{2,1,0:T(8,128)} %bitcast.14, f32[2,16,128]{2,1,0:T(8,128)} %constant.11.clone.a_3_.tw_ref, bf16[4,256,256]{2,1,0:T(8,128)(2,1)} %constant.10.clone.a_4_.w_ref, ...), custom_call_target="tpu_custom_call" | custom-call | flops 1000000000 | bytes 1048576 | tf_op jit(solution)/shard_map/receiver_side/pallas_call | solution.py:320
  3.9 0.0 copy-start
  3.9 0.0 copy-start.1
  3.9 0.0 copy-start.2
  3.9 32.3 %all_to_all.10 = f32[64,16,128]{2,1,0:T(8,128)S(1)} all-to-all(f32[64,16,128]{2,1,0:T(8,128)S(1)} %bitcast.11), channel_id=1, replica_groups=mesh['freq'=8,'row'=64] {'row'}, dimensions={0} | all-to-all | bytes 1048576 | tf_op jit(solution)/shard_map/all_to_all | solution.py:346
  36.2 0.0 copy-start.3
  36.2 0.0 copy-done
  36.2 0.0 copy-done.1
  36.2 0.0 copy-done.2
  36.2 0.7 %copy-done.3 = f32[2,16]{1,0:T(2,128)S(1)} copy-done((f32[2,16]{1,0:T(2,128)S(1)}, f32[2,16]{1,0:T(2,128)}, u32[]{:S(2)}) %copy-start.3) | copy-done | bytes 152
  36.8 4.1 %shot_side.1 = (f32[2,2,16,32,128]{4,3,2,1,0:T(8,128)S(1)}, f32[8,32,128]{2,1,0:T(8,128)}) custom-call(f32[2,16]{1,0:T(2,128)S(1)} %copy-done.3, f32[1024,128]{1,0:T(8,128)S(1)} %bitcast.10, f32[2,2,16,128]{3,2,1,0:T(8,128)S(1)} %get-tuple-element.7.corr_ref, bf16[4,256,256]{2,1,0:T(8,128)(2,1)S(1)} %copy-done, f32[2,16,128]{2,1,0:T(8,128)S(1)} %copy-done.2, ...), custom_call_target="tpu_custom_call" | custom-call | flops 1000000000 | bytes 1048576 | tf_op jit(solution)/shard_map/shot_side/pallas_call | solution.py:347
  41.0 8.8 %all-to-all-start.1 = ((f32[8,32,128]{2,1,0:T(8,128)}), f32[8,32,128]{2,1,0:T(8,128)S(1)}, u32[]{:S(2)}, u32[]{:S(2)}) async-start(f32[8,32,128]{2,1,0:T(8,128)} %get-tuple-element.9), calls=%async_computation.1 | async-start | bytes 262144 | tf_op jit(solution)/shard_map/all_to_all | solution.py:361
  49.8 1.2 %shot_side_end.1 = f32[2,32,2048]{2,1,0:T(8,128)} custom-call(f32[2,2,16,32,128]{4,3,2,1,0:T(8,128)S(1)} %get-tuple-element.8.parts_ref, f32[2,2,16,128]{3,2,1,0:T(8,128)S(1)} %get-tuple-element.7.corr_ref), custom_call_target="tpu_custom_call" | custom-call | flops 100000000 | bytes 1048576 | tf_op jit(solution)/shard_map/shot_side_end/pallas_call | solution.py:362
  51.0 6.8 %all-to-all-done.1 = f32[8,32,128]{2,1,0:T(8,128)S(1)} async-done(((f32[8,32,128]{2,1,0:T(8,128)}), f32[8,32,128]{2,1,0:T(8,128)S(1)}, u32[]{:S(2)}, u32[]{:S(2)}) %all-to-all-start.1) | async-done | bytes 131104 | tf_op jit(solution)/shard_map/all_to_all | solution.py:361
  57.8 0.6 %reduce_sum.9 = f32[32,128]{1,0:T(8,128)} reduce(f32[8,32,128]{2,1,0:T(8,128)S(1)} %all-to-all-done.1, f32[]{:T(128)} %constant.4.clone.1), dimensions={0}, to_apply=%region_0.0 | reduce | flops 28672 | bytes 147460 | tf_op jit(solution)/shard_map/reduce_sum | solution.py:371
Async XLA Ops:
  3.9 32.3 %copy-start = (bf16[4,256,256]{2,1,0:T(8,128)(2,1)S(1)}, bf16[4,256,256]{2,1,0:T(8,128)(2,1)}, u32[]{:S(2)}) copy-start(bf16[4,256,256]{2,1,0:T(8,128)(2,1)} %constant.10.clone.a_4_.w_ref) | copy-start | bytes 1572868
  3.9 32.3 %copy-start.1 = (f32[8,2,2,16,128]{4,3,2,1,0:T(8,128)S(1)}, f32[8,2,2,16,128]{4,3,2,1,0:T(8,128)}, u32[]{:S(2)}) copy-start(f32[8,2,2,16,128]{4,3,2,1,0:T(8,128)} %constant.12.clone.a_5_.e_all) | copy-start | bytes 786436
  3.9 32.3 %copy-start.2 = (f32[2,16,128]{2,1,0:T(8,128)S(1)}, f32[2,16,128]{2,1,0:T(8,128)}, u32[]{:S(2)}) copy-start(f32[2,16,128]{2,1,0:T(8,128)} %constant.11.clone.a_3_.tw_ref) | copy-start | bytes 49156
  36.2 0.7 %copy-start.3 = (f32[2,16]{1,0:T(2,128)S(1)}, f32[2,16]{1,0:T(2,128)}, u32[]{:S(2)}) copy-start(f32[2,16]{1,0:T(2,128)} %constant.13.clone.root_ref) | copy-start | bytes 388
  41.0 16.8 %all-to-all-start.1 = ((f32[8,32,128]{2,1,0:T(8,128)}), f32[8,32,128]{2,1,0:T(8,128)S(1)}, u32[]{:S(2)}, u32[]{:S(2)}) async-start(f32[8,32,128]{2,1,0:T(8,128)} %get-tuple-element.9), calls=%async_computation.1 | async-start | bytes 262144 | tf_op jit(solution)/shard_map/all_to_all | solution.py:361

commit v3 on v2

v3 whole, which is shorter than its diff:
```python
import math

import jax
import jax.numpy as jnp
import ml_dtypes
import numpy as np
from jax import lax
from jax.experimental import pallas as pl
from jax.experimental.pallas import tpu as pltpu
from jax.sharding import PartitionSpec as P

HOFF = 128
NX = 2048
NL = 16
BLOCK = 32
HIGH = 16
PAIRS = 32
LANES = 128

depth_step = 0.0125
grid_step = 0.0125
slow_slow = 1.0 / 1.5
slow_fast = 1.0 / 4.5
refs = (slow_slow, slow_fast)


def split16(table):
    high = table.astype(np.float32).astype(ml_dtypes.bfloat16)
    low = (table - high.astype(np.float64)).astype(np.float32).astype(ml_dtypes.bfloat16)
    return high, low


def real_form(matrix):
    return np.block([[matrix.real, matrix.imag], [-matrix.imag, matrix.real]])


def fourier(count):
    index = np.arange(count)
    return np.exp(-2j * math.pi * (index[:, None] * index[None, :] % count) / count)


def receiver_weights():
    forward = fourier(LANES)
    return np.stack([split16(forward.real), split16(-forward.imag)], axis=1)


def shot_weights():
    forward = fourier(64)
    same = np.eye(2)
    into = np.einsum("bsk,hg->bhsgk", forward.reshape(2, 32, 64), same).reshape(LANES, LANES)
    back = np.einsum("ks,hg->hkgs", forward.conj(), same).reshape(LANES, LANES)
    out = []
    for high, low in (split16(real_form(into)), split16(real_form(back))):
        out.append(np.concatenate([high, high, low]))
    return np.stack(out)


def twiddle_rows(count, position):
    angle = -2.0 * math.pi * np.arange(count)[:, None] * position[None, :] / NX
    return np.stack([np.cos(angle), np.sin(angle)]).astype(np.float32)


def shot_twiddles():
    lane = np.arange(LANES)
    into = twiddle_rows(PAIRS, lane // 64 * 32 + lane % 32)
    back = twiddle_rows(PAIRS, lane % 64)
    roots = twiddle_rows(PAIRS, np.full(LANES, -NX // PAIRS))
    return np.stack([into, back, roots])


def omega_of(index, total):
    return 2.0 * math.pi * (5.0 + 30.0 * (index + 0.5) / total)


def propagators(total):
    index = np.arange(NX)
    knum = np.where(index < NX // 2, index, index - NX) * (2.0 * math.pi / (NX * grid_step))
    wide = np.zeros((total, 2, 2, HIGH, LANES), np.float32)
    paired = np.zeros((total, 2, 2, PAIRS, LANES), np.float32)
    for f in range(total):
        for j in range(2):
            quad = (omega_of(f, total) * refs[j]) ** 2 - knum**2
            mag = np.exp(-depth_step * np.sqrt(np.maximum(-quad, 0.0)))
            phase = -depth_step * np.sqrt(np.maximum(quad, 0.0))
            for c, values in enumerate((mag * np.cos(phase), mag * np.sin(phase))):
                wide[f, j, c] = values.reshape(LANES, HIGH).T
                paired[f, j, c] = np.tile(values.reshape(64, PAIRS).T, (1, 2))
    return wide, paired


def add(a, b):
    return a[0] + b[0], a[1] + b[1]


def sub(a, b):
    return a[0] - b[0], a[1] - b[1]


def mul(a, b):
    return a[0] * b[0] - a[1] * b[1], a[0] * b[1] + a[1] * b[0]


def mul_conj(a, b):
    return a[0] * b[0] + a[1] * b[1], a[1] * b[0] - a[0] * b[1]


def fft4(x, sign):
    t0, t1 = add(x[0], x[2]), sub(x[0], x[2])
    t2, t3 = add(x[1], x[3]), sub(x[1], x[3])
    up = (t1[0] - t3[1], t1[1] + t3[0])
    down = (t1[0] + t3[1], t1[1] - t3[0])
    if sign < 0:
        up, down = down, up
    return [add(t0, t2), up, sub(t0, t2), down]


def turn(x, step, count, sign):
    eighths = 8 * (step % count)
    if eighths == 0:
        return x
    if eighths == 2 * count:
        return (x[1], -x[0]) if sign < 0 else (-x[1], x[0])
    if eighths == count:
        root = math.sqrt(0.5)
        if sign < 0:
            return (x[0] + x[1]) * root, (x[1] - x[0]) * root
        return (x[0] - x[1]) * root, (x[1] + x[0]) * root
    angle = sign * 2.0 * math.pi * step / count
    return mul(x, (math.cos(angle), math.sin(angle)))


def fft(x, sign):
    count = len(x)
    if count == 1:
        return x
    if count == 2:
        return [add(x[0], x[1]), sub(x[0], x[1])]
    if count == 4:
        return fft4(x, sign)
    first = 4 if count > 8 else 2
    second = count // first
    parts = [fft([x[second * m + n] for m in range(first)], sign) for n in range(second)]
    out = [None] * count
    for k in range(first):
        column = fft([turn(parts[n][k], n * k, count, sign) for n in range(second)], sign)
        for m in range(second):
            out[k + first * m] = column[m]
    return out


def halves(x):
    high = x.astype(jnp.bfloat16)
    return high, (x - high.astype(jnp.float32)).astype(jnp.bfloat16)


def dot3(x, w):
    high, low = halves(x)
    return jnp.dot(jnp.concatenate([high, low, high], axis=1), w, preferred_element_type=jnp.float32)


def row(ref, i):
    return ref[pl.ds(i, 1), :]


def scatter_up(x, tw, out_ref, rows, at):
    for k, tile in enumerate(fft(x, -1)):
        turned = mul(tile, (row(tw.at[0], k), row(tw.at[1], k)))
        for c in range(2):
            out_ref[rows * k + at : rows * k + at + 8, LANES * c : LANES * (c + 1)] = turned[c]


def middle(in_ref, rows, w_ref, e_ref, tw, out_ref):
    count = in_ref.shape[0] // rows
    spec = dot3(in_ref[...], w_ref[0])
    for j in range(2):
        moved = []
        for k in range(count):
            part = spec[k * rows : (k + 1) * rows]
            e = (row(e_ref.at[0, j, 0], k), row(e_ref.at[0, j, 1], k))
            moved.append(jnp.concatenate(mul((part[:, :LANES], part[:, LANES:]), e), axis=1))
        back = dot3(jnp.concatenate(moved, axis=0), w_ref[1])
        for k in range(count):
            part = back[k * rows : (k + 1) * rows]
            turn_back = (row(tw.at[0], k), row(tw.at[1], k))
            turned = mul_conj((part[:, :LANES], part[:, LANES:]), turn_back)
            for c in range(2):
                out_ref[j, c, k] = turned[c]


def gather_up(tiles_of, corr_of):
    result = None
    for j in range(2):
        terms = [mul(v, corr_of(j, a)) for a, v in enumerate(fft(tiles_of(j), 1))]
        result = terms if result is None else [add(r, t) for r, t in zip(result, terms)]
    return result


def corrections(index, slow_ref, omega):
    slowness = jnp.zeros(index.shape, jnp.float32)
    for layer in range(NL):
        slowness = jnp.where(index == layer, slow_ref[layer], slowness)
    upper = (slow_slow - slowness) / (slow_slow - slow_fast)
    weights = (1.0 - upper, upper)
    out = []
    for j in range(2):
        angle = -omega * depth_step * (slowness - refs[j])
        scale = weights[j] * (1.0 / NX)
        out.append((scale * jnp.cos(angle), scale * jnp.sin(angle)))
    return out


def exchange(x, y, mask, width):
    return (
        jnp.where(mask, x, pltpu.roll(y, width, 1)),
        jnp.where(mask, pltpu.roll(x, LANES - width, 1), y),
    )


def lanes_of(rows):
    return lax.broadcasted_iota(jnp.int32, (rows, LANES), 1)


def first_kernel(
    total, slow_hbm, index_hbm, field_hbm, tw_hbm, w_hbm, e_hbm, out_ref, corr_ref,
    slow_ref, index_ref, field_ref, tw_ref, wave_ref, e_ref, own_ref, w_ref, mid_ref, back_ref, sunk, sems,
):
    freq = lax.axis_index("freq")
    pairs = [
        (slow_hbm, slow_ref),
        (index_hbm, index_ref),
        (tw_hbm, tw_ref),
        (w_hbm, wave_ref),
        (e_hbm.at[pl.ds(freq, 1)], e_ref),
    ]
    for at in range(0, BLOCK, 8):
        pairs.append((field_hbm.at[:, pl.ds(at, 8)], field_ref.at[:, pl.ds(at, 8)]))
    copies = [pltpu.make_async_copy(s, d, sems.at[i]) for i, (s, d) in enumerate(pairs)]
    for copy in copies:
        copy.start()
    copies[0].wait()
    copies[1].wait()
    omega = 2.0 * math.pi * (5.0 + 30.0 * (freq.astype(jnp.float32) + 0.5) / total)
    left = lanes_of(HIGH) < 64
    for j, values in enumerate(corrections(index_ref[...], slow_ref, omega)):
        for c in range(2):
            own_ref[j, c] = values[c]
            other = pltpu.roll(values[c], 64, 1)
            corr_ref[j, c, 0] = jnp.where(left, values[c], other)
            corr_ref[j, c, 1] = jnp.where(left, other, values[c])
    copies[2].wait()
    copies[3].wait()
    copies[4].wait()
    for part, level in enumerate((0, 0, 1)):
        for way, sign in enumerate((1, -1)):
            cos, sin = wave_ref[level, 0], wave_ref[level, 1] * sign
            for at, blocks in enumerate(((cos, -sin), (sin, cos))):
                for c in range(2):
                    base = 256 * part + LANES * at
                    w_ref[way, base : base + LANES, LANES * c : LANES * (c + 1)] = blocks[c]
    for i, at in enumerate(range(0, BLOCK, 8)):
        copies[5 + i].wait()
        x = [
            tuple(field_ref[c, at : at + 8, LANES * a : LANES * (a + 1)] for c in range(2))
            for a in range(HIGH)
        ]
        scatter_up(x, tw_ref, mid_ref, BLOCK, at)
    middle(mid_ref, BLOCK, w_ref, e_ref, tw_ref, back_ref)
    for at in range(0, BLOCK, 8):
        u = gather_up(
            lambda j: [tuple(back_ref[j, c, k, at : at + 8, :] for c in range(2)) for k in range(HIGH)],
            lambda j, a: (row(own_ref.at[j, 0], a), row(own_ref.at[j, 1], a)),
        )
        for a in range(HIGH):
            for c in range(2):
                base = c * 64 + (a % 2) * 32 + at
                sunk[a // 2, base : base + 8, :] = u[a][c]
    even = (lanes_of(16) & 63) < 32
    for p in range(HIGH // 2):
        turned = sunk[p].T
        for q in range(4):
            first, second = exchange(turned[32 * q : 32 * q + 16], turned[32 * q + 16 : 32 * q + 32], even, 32)
            out_ref[p * 128 + 16 * q : p * 128 + 16 * q + 16, :] = first
            out_ref[p * 128 + 64 + 16 * q : p * 128 + 80 + 16 * q, :] = second


def second_kernel(in_ref, corr_ref, w_ref, tw_ref, e_all, parts_ref, image_hbm, mid_ref, image_ref, sems):
    e_ref = e_all.at[pl.ds(lax.axis_index("freq"), 1)]
    left = lanes_of(8) < 64
    for at in (0, 8):
        x = []
        for m in range(PAIRS):
            first, second = (in_ref[32 * m + 16 * i + at : 32 * m + 16 * i + at + 8, :] for i in range(2))
            x.append(exchange(first, second, left, 64))
        scatter_up(x, tw_ref.at[0], mid_ref, 16, at)
    middle(mid_ref, 16, w_ref, e_ref, tw_ref.at[1], parts_ref)
    start = (lax.axis_index("row") * BLOCK + NX - HOFF // 2) & (NX - 1)
    offset = start & 63
    strips = []
    for i in range(3):
        m = ((start >> 6) + i) & (PAIRS - 1)
        strip = None
        for j in range(2):
            here = None
            for k in range(PAIRS):
                at = (m * k) & (PAIRS - 1)
                root = (row(tw_ref.at[2, 0], at), row(tw_ref.at[2, 1], at))
                term = mul((parts_ref[j, 0, k], parts_ref[j, 1, k]), root)
                here = term if here is None else add(here, term)
            c = (row(corr_ref.at[j, 0, m & 1], m >> 1), row(corr_ref.at[j, 1, m & 1], m >> 1))
            term = here[0] * c[0] - here[1] * c[1]
            strip = term if strip is None else strip + term
        strips.append(strip)
    left = lanes_of(16) < 64
    bands = zip(exchange(strips[0], strips[1], left, 64), (strips[2], pltpu.roll(strips[2], 64, 1)))
    line = lax.broadcasted_iota(jnp.int32, (8, LANES), 0)
    lane = lanes_of(8)
    for h, (near, far) in enumerate(bands):
        for at in (0, 8):
            image = None
            for i in range(8):
                width = offset + 16 * h + at + i
                back = (LANES - width) & (LANES - 1)
                moved = jnp.where(
                    lane < LANES - width,
                    pltpu.roll(near[at : at + 8], back, 1),
                    pltpu.roll(far[at : at + 8], back, 1),
                )
                image = moved if image is None else jnp.where(line == i, moved, image)
            image_ref[16 * h + at : 16 * h + at + 8, :] = image
    copies = [
        pltpu.make_async_copy(image_ref, image_hbm.at[f], sems.at[f]) for f in range(image_hbm.shape[0])
    ]
    for copy in copies:
        copy.start()
    for copy in copies:
        copy.wait()


def third_kernel(parts_ref, corr_ref, out_ref):
    left = lanes_of(8) < 64
    for at in (0, 8):
        u = gather_up(
            lambda j: [tuple(parts_ref[j, c, k, at : at + 8, :] for c in range(2)) for k in range(PAIRS)],
            lambda j, m: tuple(row(corr_ref.at[j, c, m % 2], m // 2) for c in range(2)),
        )
        for a in range(HIGH):
            for c in range(2):
                for h, tile in enumerate(exchange(u[2 * a][c], u[2 * a + 1][c], left, 64)):
                    out_ref[c, 16 * h + at : 16 * h + at + 8, LANES * a : LANES * (a + 1)] = tile


def on_device(field, layer_index, layer_slowness):
    total = lax.axis_size("freq")
    groups = lax.axis_size("row")
    wide, paired = (jnp.asarray(table) for table in propagators(total))
    twiddles = jnp.asarray(twiddle_rows(HIGH, np.arange(LANES)))
    shape = lambda *dims: jax.ShapeDtypeStruct(dims, jnp.float32)
    keep = lambda *dims: pltpu.VMEM(dims, jnp.float32)
    vmem = pl.BlockSpec(memory_space=pltpu.VMEM)
    hbm = pl.BlockSpec(memory_space=pltpu.HBM)
    stay = lambda x: pltpu.with_memory_space_constraint(x, pltpu.HBM)
    near = lambda x: pltpu.with_memory_space_constraint(x, pltpu.VMEM)
    params = pltpu.CompilerParams(vmem_limit_bytes=32 * 2**20)
    cost = lambda n: pl.CostEstimate(flops=n, bytes_accessed=2**20, transcendentals=0)
    chunks, corr = pl.pallas_call(
        lambda *a: first_kernel(total, *a),
        out_shape=(keep(16 * groups, LANES), keep(2, 2, 2, HIGH, LANES)),
        in_specs=[hbm] * 6,
        out_specs=(vmem, vmem),
        scratch_shapes=[
            pltpu.SMEM((NL,), jnp.float32),
            pltpu.VMEM((HIGH, LANES), jnp.int32),
            pltpu.VMEM((2, BLOCK, NX), jnp.float32),
            pltpu.VMEM((2, HIGH, LANES), jnp.float32),
            pltpu.VMEM((2, 2, LANES, LANES), jnp.bfloat16),
            pltpu.VMEM((1, 2, 2, HIGH, LANES), jnp.float32),
            pltpu.VMEM((2, 2, HIGH, LANES), jnp.float32),
            pltpu.VMEM((2, 768, 256), jnp.bfloat16),
            pltpu.VMEM((512, 256), jnp.float32),
            pltpu.VMEM((2, 2, HIGH, BLOCK, LANES), jnp.float32),
            pltpu.VMEM((HIGH // 2, LANES, LANES), jnp.float32),
            pltpu.SemaphoreType.DMA((9,)),
        ],
        compiler_params=params,
        cost_estimate=cost(10**9),
        name="receiver_side",
    )(
        stay(layer_slowness),
        stay(layer_index.reshape(HIGH, LANES)),
        stay(field.reshape(2, BLOCK, NX)),
        stay(twiddles),
        stay(jnp.asarray(receiver_weights())),
        stay(wide),
    )
    arrived = lax.all_to_all(chunks.reshape(groups, 16, LANES), "row", 0, 0, tiled=True)
    parts, image = pl.pallas_call(
        second_kernel,
        out_shape=(keep(2, 2, PAIRS, 16, LANES), pltpu.HBM((total, BLOCK, HOFF), jnp.float32)),
        in_specs=[vmem] * 5,
        out_specs=(vmem, hbm),
        scratch_shapes=[
            pltpu.VMEM((512, 256), jnp.float32),
            pltpu.VMEM((BLOCK, LANES), jnp.float32),
            pltpu.SemaphoreType.DMA((total,)),
        ],
        compiler_params=params,
        cost_estimate=cost(10**9),
        name="shot_side",
    )(
        near(arrived.reshape(16 * groups, LANES)),
        near(corr),
        jnp.asarray(shot_weights()),
        jnp.asarray(shot_twiddles()),
        paired,
    )
    images = lax.all_to_all(image, "freq", 0, 0, tiled=True)
    sunk = pl.pallas_call(
        third_kernel,
        out_shape=shape(2, BLOCK, NX),
        in_specs=[vmem, vmem],
        out_specs=vmem,
        compiler_params=params,
        cost_estimate=cost(10**8),
        name="shot_side_end",
    )(near(parts), near(corr))
    image = jnp.swapaxes(jnp.sum(images, axis=0), 0, 1)
    return jnp.swapaxes(sunk, 1, 2)[:, None], image


def solution(mesh):
    return jax.shard_map(
        on_device,
        mesh=mesh,
        in_specs=(P(None, "freq", "row", None), P(), P()),
        out_specs=(P(None, "freq", None, "row"), P(None, "row")),
        check_vma=False,
    )
```

time: 58.7 us -> 55.9 us (0.952)
  Pallas kernels: 8.57 us -> 6.58 us
  local copies, waits for them, and re-layouts: 0.69 us -> 0.02 us
    pallas_call x1, Pallas kernels: 4.15 us -> 2.35 us  [on_device(): pl.pallas_call(second_kernel, out_shape=(keep(2, 2, PAIRS, 16, LANES), pl...]
    unnamed x8 -> x6, local copies, waits for them, and re-layouts: 0.69 us -> 0.02 us
where the time goes in v3:
time: 55.9 us; the launch traced here: 55.7 us
  blocking collectives  32.3 us (58%)
  starting transfers between devices  8.8 us (16%)
  waiting for transfers between devices  6.69 us (12%)
  Pallas kernels  6.58 us (12%)
  between operations  0.68 us (1%)
  other arithmetic  0.62 us (1%)
    all_to_all x1, blocking collectives, on_device(): lax.all_to_all(chunks.reshape(groups, 16, LANES), 'row', 0, 0, tiled=True)  32.3 us
    all_to_all x1, starting transfers between devices, on_device(): images = lax.all_to_all(image, 'freq', 0, 0, tiled=True)  8.8 us
    all_to_all x1, waiting for transfers between devices, on_device(): images = lax.all_to_all(image, 'freq', 0, 0, tiled=True)  6.69 us
    pallas_call x1, Pallas kernels, on_device(): pl.pallas_call(lambda *a: first_kernel(total, *a), out_shape=(keep(16 * g...  2.91 us
    pallas_call x1, Pallas kernels, on_device(): pl.pallas_call(second_kernel, out_shape=(keep(2, 2, PAIRS, 16, LANES), pl...  2.35 us
    pallas_call x1, Pallas kernels, on_device(): pl.pallas_call(third_kernel, out_shape=shape(2, BLOCK, NX), in_specs=[vme...  1.33 us
  transfers between devices with their start and end apart: 1, of which 1 were waited for; matrix products, arithmetic and copies ran while one was open for 0% of the time, Pallas kernels for 2%

profile of v3, /device:TPU:1, one launch (start us, length us, event | category | flops | bytes accessed | tf_op | source)
XLA Modules:
  0.0 55.7 jit_solution(13157878349906874964)
XLA Ops:
  0.6 0.0 copy-start.1
  0.6 2.9 %receiver_side.1 = (f32[1024,128]{1,0:T(8,128)S(1)}, f32[2,2,2,16,128]{4,3,2,1,0:T(8,128)S(1)}) custom-call(f32[16]{0:T(128)} %a_0_.1, s32[16,128]{1,0:T(8,128)} %bitcast.15, f32[2,32,2048]{2,1,0:T(8,128)} %bitcast.14, f32[2,16,128]{2,1,0:T(8,128)} %constant.16.clone.a_3_, bf16[2,2,128,128]{3,2,1,0:T(8,128)(2,1)} %constant.17.clone.a_4_, ...), custom_call_target="tpu_custom_call" | custom-call | flops 1000000000 | bytes 1048576 | tf_op jit(solution)/shard_map/receiver_side/pallas_call | solution.py:365
  3.6 0.0 copy-start
  3.6 0.0 copy-start.2
  3.6 32.3 %all_to_all.10 = f32[64,16,128]{2,1,0:T(8,128)S(1)} all-to-all(f32[64,16,128]{2,1,0:T(8,128)S(1)} %bitcast.11), channel_id=1, replica_groups=mesh['freq'=8,'row'=64] {'row'}, dimensions={0} | all-to-all | bytes 1048576 | tf_op jit(solution)/shard_map/all_to_all | solution.py:395
  35.8 0.0 copy-done.1
  35.8 0.0 copy-done
  35.9 0.0 copy-done.2
  35.9 2.3 %shot_side.1 = (f32[2,2,32,16,128]{4,3,2,1,0:T(8,128)S(1)}, f32[8,32,128]{2,1,0:T(8,128)}) custom-call(f32[1024,128]{1,0:T(8,128)S(1)} %bitcast.10, f32[2,2,2,16,128]{4,3,2,1,0:T(8,128)S(1)} %get-tuple-element.7.corr_ref, bf16[2,768,256]{2,1,0:T(8,128)(2,1)S(1)} %copy-done, f32[3,2,32,128]{3,2,1,0:T(8,128)S(1)} %copy-done.2, f32[8,2,2,32,128]{4,3,2,1,0:T(8,128)S(1)} %copy-done.1), custom_call_target="tpu_custom_call" | custom-call | flops 1000000000 | bytes 1048576 | tf_op jit(solution)/shard_map/shot_side/pallas_call | solution.py:396
  38.2 8.8 %all-to-all-start.1 = ((f32[8,32,128]{2,1,0:T(8,128)}), f32[8,32,128]{2,1,0:T(8,128)S(1)}, u32[]{:S(2)}, u32[]{:S(2)}) async-start(f32[8,32,128]{2,1,0:T(8,128)} %get-tuple-element.9), calls=%async_computation.1 | async-start | bytes 262144 | tf_op jit(solution)/shard_map/all_to_all | solution.py:416
  47.0 1.3 %shot_side_end.1 = f32[2,32,2048]{2,1,0:T(8,128)} custom-call(f32[2,2,32,16,128]{4,3,2,1,0:T(8,128)S(1)} %get-tuple-element.8.parts_ref, f32[2,2,2,16,128]{4,3,2,1,0:T(8,128)S(1)} %get-tuple-element.7.corr_ref), custom_call_target="tpu_custom_call" | custom-call | flops 100000000 | bytes 1048576 | tf_op jit(solution)/shard_map/shot_side_end/pallas_call | solution.py:417
  48.3 6.7 %all-to-all-done.1 = f32[8,32,128]{2,1,0:T(8,128)S(1)} async-done(((f32[8,32,128]{2,1,0:T(8,128)}), f32[8,32,128]{2,1,0:T(8,128)S(1)}, u32[]{:S(2)}, u32[]{:S(2)}) %all-to-all-start.1) | async-done | bytes 131104 | tf_op jit(solution)/shard_map/all_to_all | solution.py:416
  55.0 0.6 %reduce_sum.9 = f32[32,128]{1,0:T(8,128)} reduce(f32[8,32,128]{2,1,0:T(8,128)S(1)} %all-to-all-done.1, f32[]{:T(128)} %constant.6.clone.1), dimensions={0}, to_apply=%region_0.0 | reduce | flops 28672 | bytes 147460 | tf_op jit(solution)/shard_map/reduce_sum | solution.py:426
Async XLA Ops:
  0.6 35.2 %copy-start.1 = (f32[8,2,2,32,128]{4,3,2,1,0:T(8,128)S(1)}, f32[8,2,2,32,128]{4,3,2,1,0:T(8,128)}, u32[]{:S(2)}) copy-start(f32[8,2,2,32,128]{4,3,2,1,0:T(8,128)} %constant.15.clone.e_all) | copy-start | bytes 1572868
  3.6 32.3 %copy-start = (bf16[2,768,256]{2,1,0:T(8,128)(2,1)S(1)}, bf16[2,768,256]{2,1,0:T(8,128)(2,1)}, u32[]{:S(2)}) copy-start(bf16[2,768,256]{2,1,0:T(8,128)(2,1)} %constant.18.clone.w_ref) | copy-start | bytes 2359300
  3.6 32.3 %copy-start.2 = (f32[3,2,32,128]{3,2,1,0:T(8,128)S(1)}, f32[3,2,32,128]{3,2,1,0:T(8,128)}, u32[]{:S(2)}) copy-start(f32[3,2,32,128]{3,2,1,0:T(8,128)} %constant.19.clone.tw_ref) | copy-start | bytes 294916
  38.2 16.8 %all-to-all-start.1 = ((f32[8,32,128]{2,1,0:T(8,128)}), f32[8,32,128]{2,1,0:T(8,128)S(1)}, u32[]{:S(2)}, u32[]{:S(2)}) async-start(f32[8,32,128]{2,1,0:T(8,128)} %get-tuple-element.9), calls=%async_computation.1 | async-start | bytes 262144 | tf_op jit(solution)/shard_map/all_to_all | solution.py:416

commit v4 on v3

--- a/solution.py
+++ b/solution.py
@@ -64,8 +64,16 @@
     lane = np.arange(LANES)
     into = twiddle_rows(PAIRS, lane // 64 * 32 + lane % 32)
     back = twiddle_rows(PAIRS, lane % 64)
-    roots = twiddle_rows(PAIRS, np.full(LANES, -NX // PAIRS))
-    return np.stack([into, back, roots])
+    return np.stack([into, back])
+
+
+def window_twiddles():
+    lane = np.arange(LANES) % 64
+    return np.stack([twiddle_rows(PAIRS, lane + 64 * m) for m in range(PAIRS)])
+
+
+def window_start():
+    return (lax.axis_index("row") * BLOCK + NX - HOFF // 2) & (NX - 1)
 
 
 def omega_of(index, total):
@@ -179,12 +187,26 @@
             e = (row(e_ref.at[0, j, 0], k), row(e_ref.at[0, j, 1], k))
             moved.append(jnp.concatenate(mul((part[:, :LANES], part[:, LANES:]), e), axis=1))
         back = dot3(jnp.concatenate(moved, axis=0), w_ref[1])
+        tiles = []
         for k in range(count):
             part = back[k * rows : (k + 1) * rows]
-            turn_back = (row(tw.at[0], k), row(tw.at[1], k))
-            turned = mul_conj((part[:, :LANES], part[:, LANES:]), turn_back)
+            tiles.append((part[:, :LANES], part[:, LANES:]))
+            turned = mul_conj(tiles[k], (row(tw.at[0], k), row(tw.at[1], k)))
             for c in range(2):
                 out_ref[j, c, k] = turned[c]
+        yield j, tiles
+
+
+def window_tiles(tiles, tw):
+    sums = [None] * 3
+    for k in range(8):
+        part = [mul_conj(tiles[k + n], (row(tw.at[0], k + n), row(tw.at[1], k + n))) for n in range(0, 32, 8)]
+        even = add(part[0], part[2]), add(part[1], part[3])
+        odd = sub(part[0], part[2]), sub(part[1], part[3])
+        odd = (odd[0][0] - odd[1][1], odd[0][1] + odd[1][0])
+        terms = (add(*even), turn(odd, k, 32, 1), turn(sub(*even), k, 16, 1))
+        sums = [t if p is None else add(p, t) for p, t in zip(sums, terms)]
+    return sums
 
 
 def gather_up(tiles_of, corr_of):
@@ -216,12 +238,27 @@
     )
 
 
+def place(block):
+    return (3 * (block // 8) % 8) * 8 + block % 8
+
+
+def row_order(groups):
+    order = [0] * groups
+    for block in range(groups):
+        order[place(block)] = block
+    return order
+
+
+def freq_order(total):
+    return [3 * i % total for i in range(total)]
+
+
 def lanes_of(rows):
     return lax.broadcasted_iota(jnp.int32, (rows, LANES), 1)
 
 
 def first_kernel(
-    total, slow_hbm, index_hbm, field_hbm, tw_hbm, w_hbm, e_hbm, out_ref, corr_ref,
+    total, slow_hbm, index_hbm, field_hbm, tw_hbm, w_hbm, e_hbm, window_hbm, out_ref, corr_ref, window_ref,
     slow_ref, index_ref, field_ref, tw_ref, wave_ref, e_ref, own_ref, w_ref, mid_ref, back_ref, sunk, sems,
 ):
     freq = lax.axis_index("freq")
@@ -234,6 +271,7 @@
     ]
     for at in range(0, BLOCK, 8):
         pairs.append((field_hbm.at[:, pl.ds(at, 8)], field_ref.at[:, pl.ds(at, 8)]))
+    pairs.append((window_hbm.at[window_start() >> 6], window_ref))
     copies = [pltpu.make_async_copy(s, d, sems.at[i]) for i, (s, d) in enumerate(pairs)]
     for copy in copies:
         copy.start()
@@ -264,7 +302,9 @@
             for a in range(HIGH)
         ]
         scatter_up(x, tw_ref, mid_ref, BLOCK, at)
-    middle(mid_ref, BLOCK, w_ref, e_ref, tw_ref, back_ref)
+    for _ in middle(mid_ref, BLOCK, w_ref, e_ref, tw_ref, back_ref):
+        pass
+    copies[9].wait()
     for at in range(0, BLOCK, 8):
         u = gather_up(
             lambda j: [tuple(back_ref[j, c, k, at : at + 8, :] for c in range(2)) for k in range(HIGH)],
@@ -279,37 +319,30 @@
         turned = sunk[p].T
         for q in range(4):
             first, second = exchange(turned[32 * q : 32 * q + 16], turned[32 * q + 16 : 32 * q + 32], even, 32)
-            out_ref[p * 128 + 16 * q : p * 128 + 16 * q + 16, :] = first
-            out_ref[p * 128 + 64 + 16 * q : p * 128 + 80 + 16 * q, :] = second
-
-
-def second_kernel(in_ref, corr_ref, w_ref, tw_ref, e_all, parts_ref, image_hbm, mid_ref, image_ref, sems):
+            for block, chunk in ((8 * p + q, first), (8 * p + 4 + q, second)):
+                out_ref[16 * place(block) : 16 * place(block) + 16, :] = chunk
+
+
+def second_kernel(in_ref, corr_ref, window_ref, w_ref, tw_ref, e_all, parts_ref, image_hbm, mid_ref, image_ref, sems):
     e_ref = e_all.at[pl.ds(lax.axis_index("freq"), 1)]
     left = lanes_of(8) < 64
     for at in (0, 8):
         x = []
         for m in range(PAIRS):
-            first, second = (in_ref[32 * m + 16 * i + at : 32 * m + 16 * i + at + 8, :] for i in range(2))
+            first, second = (
+                in_ref[16 * place(2 * m + i) + at : 16 * place(2 * m + i) + at + 8, :] for i in range(2)
+            )
             x.append(exchange(first, second, left, 64))
         scatter_up(x, tw_ref.at[0], mid_ref, 16, at)
-    middle(mid_ref, 16, w_ref, e_ref, tw_ref.at[1], parts_ref)
-    start = (lax.axis_index("row") * BLOCK + NX - HOFF // 2) & (NX - 1)
+    start = window_start()
     offset = start & 63
-    strips = []
-    for i in range(3):
-        m = ((start >> 6) + i) & (PAIRS - 1)
-        strip = None
-        for j in range(2):
-            here = None
-            for k in range(PAIRS):
-                at = (m * k) & (PAIRS - 1)
-                root = (row(tw_ref.at[2, 0], at), row(tw_ref.at[2, 1], at))
-                term = mul((parts_ref[j, 0, k], parts_ref[j, 1, k]), root)
-                here = term if here is None else add(here, term)
+    strips = [None] * 3
+    for j, tiles in middle(mid_ref, 16, w_ref, e_ref, tw_ref.at[1], parts_ref):
+        for i, here in enumerate(window_tiles(tiles, window_ref)):
+            m = ((start >> 6) + i) & (PAIRS - 1)
             c = (row(corr_ref.at[j, 0, m & 1], m >> 1), row(corr_ref.at[j, 1, m & 1], m >> 1))
             term = here[0] * c[0] - here[1] * c[1]
-            strip = term if strip is None else strip + term
-        strips.append(strip)
+            strips[i] = term if j == 0 else strips[i] + term
     left = lanes_of(16) < 64
     bands = zip(exchange(strips[0], strips[1], left, 64), (strips[2], pltpu.roll(strips[2], 64, 1)))
     line = lax.broadcasted_iota(jnp.int32, (8, LANES), 0)
@@ -362,11 +395,11 @@
     near = lambda x: pltpu.with_memory_space_constraint(x, pltpu.VMEM)
     params = pltpu.CompilerParams(vmem_limit_bytes=32 * 2**20)
     cost = lambda n: pl.CostEstimate(flops=n, bytes_accessed=2**20, transcendentals=0)
-    chunks, corr = pl.pallas_call(
+    chunks, corr, window = pl.pallas_call(
         lambda *a: first_kernel(total, *a),
-        out_shape=(keep(16 * groups, LANES), keep(2, 2, 2, HIGH, LANES)),
-        in_specs=[hbm] * 6,
-        out_specs=(vmem, vmem),
+        out_shape=(keep(16 * groups, LANES), keep(2, 2, 2, HIGH, LANES), keep(2, PAIRS, LANES)),
+        in_specs=[hbm] * 7,
+        out_specs=(vmem, vmem, vmem),
         scratch_shapes=[
             pltpu.SMEM((NL,), jnp.float32),
             pltpu.VMEM((HIGH, LANES), jnp.int32),
@@ -379,7 +412,7 @@
             pltpu.VMEM((512, 256), jnp.float32),
             pltpu.VMEM((2, 2, HIGH, BLOCK, LANES), jnp.float32),
             pltpu.VMEM((HIGH // 2, LANES, LANES), jnp.float32),
-            pltpu.SemaphoreType.DMA((9,)),
+            pltpu.SemaphoreType.DMA((10,)),
         ],
         compiler_params=params,
         cost_estimate=cost(10**9),
@@ -391,12 +424,13 @@
         stay(twiddles),
         stay(jnp.asarray(receiver_weights())),
         stay(wide),
+        stay(jnp.asarray(window_twiddles())),
     )
-    arrived = lax.all_to_all(chunks.reshape(groups, 16, LANES), "row", 0, 0, tiled=True)
+    arrived = lax.all_to_all(chunks.reshape(groups, 16, LANES), "row", 0, 0, tiled=True, axis_index_groups=[row_order(groups)])
     parts, image = pl.pallas_call(
         second_kernel,
         out_shape=(keep(2, 2, PAIRS, 16, LANES), pltpu.HBM((total, BLOCK, HOFF), jnp.float32)),
-        in_specs=[vmem] * 5,
+        in_specs=[vmem] * 6,
         out_specs=(vmem, hbm),
         scratch_shapes=[
             pltpu.VMEM((512, 256), jnp.float32),
@@ -409,11 +443,12 @@
     )(
         near(arrived.reshape(16 * groups, LANES)),
         near(corr),
+        near(window),
         jnp.asarray(shot_weights()),
         jnp.asarray(shot_twiddles()),
         paired,
     )
-    images = lax.all_to_all(image, "freq", 0, 0, tiled=True)
+    images = lax.all_to_all(image, "freq", 0, 0, tiled=True, axis_index_groups=[freq_order(total)])
     sunk = pl.pallas_call(
         third_kernel,
         out_shape=shape(2, BLOCK, NX),

time: 55.9 us -> 55.1 us (0.986)
  starting transfers between devices: 8.8 us -> 8.24 us
    all_to_all x1, starting transfers between devices: 8.8 us -> 8.24 us  [on_device(): lax.all_to_all(image, 'freq', 0, 0, tiled=True, axis_index_groups=[freq_o...]
where the time goes in v4:
time: 55.1 us; the launch traced here: 54.8 us
  blocking collectives  32.5 us (59%)
  starting transfers between devices  8.24 us (15%)
  waiting for transfers between devices  6.47 us (12%)
  Pallas kernels  6.3 us (11%)
  between operations  0.68 us (1%)
  other arithmetic  0.62 us (1%)
    all_to_all x1, blocking collectives, on_device(): lax.all_to_all(chunks.reshape(groups, 16, LANES), 'row', 0, 0, tiled=True...  32.5 us
    all_to_all x1, starting transfers between devices, on_device(): lax.all_to_all(image, 'freq', 0, 0, tiled=True, axis_index_groups=[freq_o...  8.24 us
    all_to_all x1, waiting for transfers between devices, on_device(): lax.all_to_all(image, 'freq', 0, 0, tiled=True, axis_index_groups=[freq_o...  6.47 us
    pallas_call x1, Pallas kernels, on_device(): pl.pallas_call(lambda *a: first_kernel(total, *a), out_shape=(keep(16 * g...  2.79 us
    pallas_call x1, Pallas kernels, on_device(): pl.pallas_call(second_kernel, out_shape=(keep(2, 2, PAIRS, 16, LANES), pl...  2.18 us
    pallas_call x1, Pallas kernels, on_device(): pl.pallas_call(third_kernel, out_shape=shape(2, BLOCK, NX), in_specs=[vme...  1.33 us
  transfers between devices with their start and end apart: 1, of which 1 were waited for; matrix products, arithmetic and copies ran while one was open for 0% of the time, Pallas kernels for 2%

profile of v4, /device:TPU:1, one launch (start us, length us, event | category | flops | bytes accessed | tf_op | source)
XLA Modules:
  0.0 54.8 jit_solution(7781418038280667071)
XLA Ops:
  0.6 0.0 copy-start.1
  0.6 2.8 %receiver_side.1 = (f32[1024,128]{1,0:T(8,128)S(1)}, f32[2,2,2,16,128]{4,3,2,1,0:T(8,128)S(1)}, f32[2,32,128]{2,1,0:T(8,128)S(1)}) custom-call(f32[16]{0:T(128)} %a_0_.1, s32[16,128]{1,0:T(8,128)} %bitcast.15, f32[2,32,2048]{2,1,0:T(8,128)} %bitcast.14, f32[2,16,128]{2,1,0:T(8,128)} %constant.18.clone.a_3_, bf16[2,2,128,128]{3,2,1,0:T(8,128)(2,1)} %constant.19.clone.a_4_, ...), custom_call_target="tpu_custom_call" | custom-call | flops 1000000000 | bytes 1048576 | tf_op jit(solution)/shard_map/receiver_side/pallas_call | solution.py:398
  3.4 0.0 copy-start
  3.5 0.0 copy-start.2
  3.5 32.5 %all_to_all.10 = f32[64,16,128]{2,1,0:T(8,128)S(1)} all-to-all(f32[64,16,128]{2,1,0:T(8,128)S(1)} %bitcast.11), channel_id=1, replica_groups={{0,1,2,3,4,5,6,7,24,25,26,27,28,29,30,31,48,49,50,51,52,53,54,55,8,9,10..., dimensions={0} | all-to-all | bytes 1048576 | tf_op jit(solution)/shard_map/all_to_all | solution.py:429
  36.0 0.0 copy-done.1
  36.0 0.0 copy-done
  36.0 0.0 copy-done.2
  36.0 2.2 %shot_side.1 = (f32[2,2,32,16,128]{4,3,2,1,0:T(8,128)S(1)}, f32[8,32,128]{2,1,0:T(8,128)}) custom-call(f32[1024,128]{1,0:T(8,128)S(1)} %bitcast.10, f32[2,2,2,16,128]{4,3,2,1,0:T(8,128)S(1)} %get-tuple-element.8.corr_ref, f32[2,32,128]{2,1,0:T(8,128)S(1)} %get-tuple-element.9.window_ref, bf16[2,768,256]{2,1,0:T(8,128)(2,1)S(1)} %copy-done, ...), custom_call_target="tpu_custom_call" | custom-call | flops 1000000000 | bytes 1048576 | tf_op jit(solution)/shard_map/shot_side/pallas_call | solution.py:430
  38.2 8.2 %all-to-all-start.1 = ((f32[8,32,128]{2,1,0:T(8,128)}), f32[8,32,128]{2,1,0:T(8,128)S(1)}, u32[]{:S(2)}, u32[]{:S(2)}) async-start(f32[8,32,128]{2,1,0:T(8,128)} %get-tuple-element.11), calls=%async_computation.1 | async-start | bytes 262144 | tf_op jit(solution)/shard_map/all_to_all | solution.py:451
  46.4 1.3 %shot_side_end.1 = f32[2,32,2048]{2,1,0:T(8,128)} custom-call(f32[2,2,32,16,128]{4,3,2,1,0:T(8,128)S(1)} %get-tuple-element.10.parts_ref, f32[2,2,2,16,128]{4,3,2,1,0:T(8,128)S(1)} %get-tuple-element.8.corr_ref), custom_call_target="tpu_custom_call" | custom-call | flops 100000000 | bytes 1048576 | tf_op jit(solution)/shard_map/shot_side_end/pallas_call | solution.py:452
  47.7 6.5 %all-to-all-done.1 = f32[8,32,128]{2,1,0:T(8,128)S(1)} async-done(((f32[8,32,128]{2,1,0:T(8,128)}), f32[8,32,128]{2,1,0:T(8,128)S(1)}, u32[]{:S(2)}, u32[]{:S(2)}) %all-to-all-start.1) | async-done | bytes 131104 | tf_op jit(solution)/shard_map/all_to_all | solution.py:451
  54.2 0.6 %reduce_sum.9 = f32[32,128]{1,0:T(8,128)} reduce(f32[8,32,128]{2,1,0:T(8,128)S(1)} %all-to-all-done.1, f32[]{:T(128)} %constant.7.clone.1), dimensions={0}, to_apply=%region_0.0 | reduce | flops 28672 | bytes 147460 | tf_op jit(solution)/shard_map/reduce_sum | solution.py:461
Async XLA Ops:
  0.6 35.4 %copy-start.1 = (f32[8,2,2,32,128]{4,3,2,1,0:T(8,128)S(1)}, f32[8,2,2,32,128]{4,3,2,1,0:T(8,128)}, u32[]{:S(2)}) copy-start(f32[8,2,2,32,128]{4,3,2,1,0:T(8,128)} %constant.17.clone.e_all) | copy-start | bytes 1572868
  3.4 32.5 %copy-start = (bf16[2,768,256]{2,1,0:T(8,128)(2,1)S(1)}, bf16[2,768,256]{2,1,0:T(8,128)(2,1)}, u32[]{:S(2)}) copy-start(bf16[2,768,256]{2,1,0:T(8,128)(2,1)} %constant.21.clone.w_ref) | copy-start | bytes 2359300
  3.5 32.5 %copy-start.2 = (f32[2,2,32,128]{3,2,1,0:T(8,128)S(1)}, f32[2,2,32,128]{3,2,1,0:T(8,128)}, u32[]{:S(2)}) copy-start(f32[2,2,32,128]{3,2,1,0:T(8,128)} %constant.22.clone.tw_ref) | copy-start | bytes 196612
  38.2 16.0 %all-to-all-start.1 = ((f32[8,32,128]{2,1,0:T(8,128)}), f32[8,32,128]{2,1,0:T(8,128)S(1)}, u32[]{:S(2)}, u32[]{:S(2)}) async-start(f32[8,32,128]{2,1,0:T(8,128)} %get-tuple-element.11), calls=%async_computation.1 | async-start | bytes 262144 | tf_op jit(solution)/shard_map/all_to_all | solution.py:451

commit v5 on v4

--- a/solution.py
+++ b/solution.py
@@ -239,7 +239,7 @@
 
 
 def place(block):
-    return (3 * (block // 8) % 8) * 8 + block % 8
+    return 11 * block % 64
 
 
 def row_order(groups):
@@ -323,7 +323,7 @@
                 out_ref[16 * place(block) : 16 * place(block) + 16, :] = chunk
 
 
-def second_kernel(in_ref, corr_ref, window_ref, w_ref, tw_ref, e_all, parts_ref, image_hbm, mid_ref, image_ref, sems):
+def second_kernel(in_ref, corr_ref, window_ref, w_ref, tw_ref, e_all, parts_ref, images_ref, mid_ref, image_ref):
     e_ref = e_all.at[pl.ds(lax.axis_index("freq"), 1)]
     left = lanes_of(8) < 64
     for at in (0, 8):
@@ -360,13 +360,8 @@
                 )
                 image = moved if image is None else jnp.where(line == i, moved, image)
             image_ref[16 * h + at : 16 * h + at + 8, :] = image
-    copies = [
-        pltpu.make_async_copy(image_ref, image_hbm.at[f], sems.at[f]) for f in range(image_hbm.shape[0])
-    ]
-    for copy in copies:
-        copy.start()
-    for copy in copies:
-        copy.wait()
+    for f in range(images_ref.shape[0]):
+        images_ref[f] = image_ref[...]
 
 
 def third_kernel(parts_ref, corr_ref, out_ref):
@@ -429,13 +424,12 @@
     arrived = lax.all_to_all(chunks.reshape(groups, 16, LANES), "row", 0, 0, tiled=True, axis_index_groups=[row_order(groups)])
     parts, image = pl.pallas_call(
         second_kernel,
-        out_shape=(keep(2, 2, PAIRS, 16, LANES), pltpu.HBM((total, BLOCK, HOFF), jnp.float32)),
+        out_shape=(keep(2, 2, PAIRS, 16, LANES), keep(total, BLOCK, HOFF)),
         in_specs=[vmem] * 6,
-        out_specs=(vmem, hbm),
+        out_specs=(vmem, vmem),
         scratch_shapes=[
             pltpu.VMEM((512, 256), jnp.float32),
             pltpu.VMEM((BLOCK, LANES), jnp.float32),
-            pltpu.SemaphoreType.DMA((total,)),
         ],
         compiler_params=params,
         cost_estimate=cost(10**9),

time: 55.1 us -> 54.3 us (0.985)
  blocking collectives: 32.5 us -> 30.6 us
  starting transfers between devices: 8.24 us -> 9.39 us
    all_to_all x1, blocking collectives: 32.5 us -> 30.6 us  [on_device(): lax.all_to_all(chunks.reshape(groups, 16, LANES), 'row', 0, 0, tiled=True...]
    all_to_all x1, starting transfers between devices: 8.24 us -> 9.39 us  [on_device(): lax.all_to_all(image, 'freq', 0, 0, tiled=True, axis_index_groups=[freq_o...]
where the time goes in v5:
time: 54.3 us; the launch traced here: 54.1 us
  blocking collectives  30.6 us (56%)
  starting transfers between devices  9.39 us (17%)
  waiting for transfers between devices  6.54 us (12%)
  Pallas kernels  6.23 us (11%)
  between operations  0.67 us (1%)
  other arithmetic  0.62 us (1%)
    all_to_all x1, blocking collectives, on_device(): lax.all_to_all(chunks.reshape(groups, 16, LANES), 'row', 0, 0, tiled=True...  30.6 us
    all_to_all x1, starting transfers between devices, on_device(): lax.all_to_all(image, 'freq', 0, 0, tiled=True, axis_index_groups=[freq_o...  9.39 us
    all_to_all x1, waiting for transfers between devices, on_device(): lax.all_to_all(image, 'freq', 0, 0, tiled=True, axis_index_groups=[freq_o...  6.54 us
    pallas_call x1, Pallas kernels, on_device(): pl.pallas_call(lambda *a: first_kernel(total, *a), out_shape=(keep(16 * g...  2.79 us
    pallas_call x1, Pallas kernels, on_device(): pl.pallas_call(second_kernel, out_shape=(keep(2, 2, PAIRS, 16, LANES), ke...  2.11 us
    pallas_call x1, Pallas kernels, on_device(): pl.pallas_call(third_kernel, out_shape=shape(2, BLOCK, NX), in_specs=[vme...  1.33 us
  transfers between devices with their start and end apart: 1, of which 1 were waited for; matrix products, arithmetic and copies ran while one was open for 0% of the time, Pallas kernels for 2%

profile of v5, /device:TPU:1, one launch (start us, length us, event | category | flops | bytes accessed | tf_op | source)
XLA Modules:
  0.0 54.1 jit_solution(16285008943024211120)
XLA Ops:
  0.6 0.0 copy-start.1
  0.6 2.8 %receiver_side.1 = (f32[1024,128]{1,0:T(8,128)S(1)}, f32[2,2,2,16,128]{4,3,2,1,0:T(8,128)S(1)}, f32[2,32,128]{2,1,0:T(8,128)S(1)}) custom-call(f32[16]{0:T(128)} %a_0_.1, s32[16,128]{1,0:T(8,128)} %bitcast.15, f32[2,32,2048]{2,1,0:T(8,128)} %bitcast.14, f32[2,16,128]{2,1,0:T(8,128)} %constant.18.clone.a_3_, bf16[2,2,128,128]{3,2,1,0:T(8,128)(2,1)} %constant.19.clone.a_4_, ...), custom_call_target="tpu_custom_call" | custom-call | flops 1000000000 | bytes 1048576 | tf_op jit(solution)/shard_map/receiver_side/pallas_call | solution.py:393
  3.4 0.0 copy-start
  3.5 0.0 copy-start.2
  3.5 30.6 %all_to_all.10 = f32[64,16,128]{2,1,0:T(8,128)S(1)} all-to-all(f32[64,16,128]{2,1,0:T(8,128)S(1)} %bitcast.11), channel_id=1, replica_groups={{0,35,6,41,12,47,18,53,24,59,30,1,36,7,42,13,48,19,54,25,60,31,2,37,8,4..., dimensions={0} | all-to-all | bytes 1048576 | tf_op jit(solution)/shard_map/all_to_all | solution.py:424
  34.0 0.0 copy-done.1
  34.0 0.0 copy-done
  34.1 0.0 copy-done.2
  34.1 2.1 %shot_side.1 = (f32[2,2,32,16,128]{4,3,2,1,0:T(8,128)S(1)}, f32[8,32,128]{2,1,0:T(8,128)}) custom-call(f32[1024,128]{1,0:T(8,128)S(1)} %bitcast.10, f32[2,2,2,16,128]{4,3,2,1,0:T(8,128)S(1)} %get-tuple-element.8.corr_ref, f32[2,32,128]{2,1,0:T(8,128)S(1)} %get-tuple-element.9.window_ref, bf16[2,768,256]{2,1,0:T(8,128)(2,1)S(1)} %copy-done, ...), custom_call_target="tpu_custom_call" | custom-call | flops 1000000000 | bytes 1048576 | tf_op jit(solution)/shard_map/shot_side/pallas_call | solution.py:425
  36.2 9.4 %all-to-all-start.1 = ((f32[8,32,128]{2,1,0:T(8,128)}), f32[8,32,128]{2,1,0:T(8,128)S(1)}, u32[]{:S(2)}, u32[]{:S(2)}) async-start(f32[8,32,128]{2,1,0:T(8,128)} %get-tuple-element.11), calls=%async_computation.1 | async-start | bytes 262144 | tf_op jit(solution)/shard_map/all_to_all | solution.py:445
  45.6 1.3 %shot_side_end.1 = f32[2,32,2048]{2,1,0:T(8,128)} custom-call(f32[2,2,32,16,128]{4,3,2,1,0:T(8,128)S(1)} %get-tuple-element.10.parts_ref, f32[2,2,2,16,128]{4,3,2,1,0:T(8,128)S(1)} %get-tuple-element.8.corr_ref), custom_call_target="tpu_custom_call" | custom-call | flops 100000000 | bytes 1048576 | tf_op jit(solution)/shard_map/shot_side_end/pallas_call | solution.py:446
  46.9 6.5 %all-to-all-done.1 = f32[8,32,128]{2,1,0:T(8,128)S(1)} async-done(((f32[8,32,128]{2,1,0:T(8,128)}), f32[8,32,128]{2,1,0:T(8,128)S(1)}, u32[]{:S(2)}, u32[]{:S(2)}) %all-to-all-start.1) | async-done | bytes 131104 | tf_op jit(solution)/shard_map/all_to_all | solution.py:445
  53.4 0.6 %reduce_sum.9 = f32[32,128]{1,0:T(8,128)} reduce(f32[8,32,128]{2,1,0:T(8,128)S(1)} %all-to-all-done.1, f32[]{:T(128)} %constant.7.clone.1), dimensions={0}, to_apply=%region_0.0 | reduce | flops 28672 | bytes 147460 | tf_op jit(solution)/shard_map/reduce_sum | solution.py:455
Async XLA Ops:
  0.6 33.4 %copy-start.1 = (f32[8,2,2,32,128]{4,3,2,1,0:T(8,128)S(1)}, f32[8,2,2,32,128]{4,3,2,1,0:T(8,128)}, u32[]{:S(2)}) copy-start(f32[8,2,2,32,128]{4,3,2,1,0:T(8,128)} %constant.17.clone.e_all) | copy-start | bytes 1572868
  3.4 30.6 %copy-start = (bf16[2,768,256]{2,1,0:T(8,128)(2,1)S(1)}, bf16[2,768,256]{2,1,0:T(8,128)(2,1)}, u32[]{:S(2)}) copy-start(bf16[2,768,256]{2,1,0:T(8,128)(2,1)} %constant.21.clone.w_ref) | copy-start | bytes 2359300
  3.5 30.6 %copy-start.2 = (f32[2,2,32,128]{3,2,1,0:T(8,128)S(1)}, f32[2,2,32,128]{3,2,1,0:T(8,128)}, u32[]{:S(2)}) copy-start(f32[2,2,32,128]{3,2,1,0:T(8,128)} %constant.22.clone.tw_ref) | copy-start | bytes 196612
  36.2 17.3 %all-to-all-start.1 = ((f32[8,32,128]{2,1,0:T(8,128)}), f32[8,32,128]{2,1,0:T(8,128)S(1)}, u32[]{:S(2)}, u32[]{:S(2)}) async-start(f32[8,32,128]{2,1,0:T(8,128)} %get-tuple-element.11), calls=%async_computation.1 | async-start | bytes 262144 | tf_op jit(solution)/shard_map/all_to_all | solution.py:445

commit v6 on v5

--- a/solution.py
+++ b/solution.py
@@ -239,7 +239,7 @@
 
 
 def place(block):
-    return 11 * block % 64
+    return 19 * block % 64
 
 
 def row_order(groups):

time: 54.3 us -> 54.5 us (level)
  no operation moved by 1% of the time
where the time goes in v6:
time: 54.5 us; the launch traced here: 53.8 us
  blocking collectives  30.8 us (57%)
  starting transfers between devices  9.15 us (17%)
  waiting for transfers between devices  6.3 us (12%)
  Pallas kernels  6.24 us (11%)
  between operations  0.67 us (1%)
  other arithmetic  0.62 us (1%)
    all_to_all x1, blocking collectives, on_device(): lax.all_to_all(chunks.reshape(groups, 16, LANES), 'row', 0, 0, tiled=True...  30.8 us
    all_to_all x1, starting transfers between devices, on_device(): lax.all_to_all(image, 'freq', 0, 0, tiled=True, axis_index_groups=[freq_o...  9.15 us
    all_to_all x1, waiting for transfers between devices, on_device(): lax.all_to_all(image, 'freq', 0, 0, tiled=True, axis_index_groups=[freq_o...  6.3 us
    pallas_call x1, Pallas kernels, on_device(): pl.pallas_call(lambda *a: first_kernel(total, *a), out_shape=(keep(16 * g...  2.79 us
    pallas_call x1, Pallas kernels, on_device(): pl.pallas_call(second_kernel, out_shape=(keep(2, 2, PAIRS, 16, LANES), ke...  2.12 us
    pallas_call x1, Pallas kernels, on_device(): pl.pallas_call(third_kernel, out_shape=shape(2, BLOCK, NX), in_specs=[vme...  1.33 us
  transfers between devices with their start and end apart: 1, of which 1 were waited for; matrix products, arithmetic and copies ran while one was open for 0% of the time, Pallas kernels for 2%

profile of v6, /device:TPU:1, one launch (start us, length us, event | category | flops | bytes accessed | tf_op | source)
XLA Modules:
  0.0 53.8 jit_solution(11109616374827444127)
XLA Ops:
  0.6 0.0 copy-start.1
  0.6 2.8 %receiver_side.1 = (f32[1024,128]{1,0:T(8,128)S(1)}, f32[2,2,2,16,128]{4,3,2,1,0:T(8,128)S(1)}, f32[2,32,128]{2,1,0:T(8,128)S(1)}) custom-call(f32[16]{0:T(128)} %a_0_.1, s32[16,128]{1,0:T(8,128)} %bitcast.15, f32[2,32,2048]{2,1,0:T(8,128)} %bitcast.14, f32[2,16,128]{2,1,0:T(8,128)} %constant.18.clone.a_3_, bf16[2,2,128,128]{3,2,1,0:T(8,128)(2,1)} %constant.19.clone.a_4_, ...), custom_call_target="tpu_custom_call" | custom-call | flops 1000000000 | bytes 1048576 | tf_op jit(solution)/shard_map/receiver_side/pallas_call | solution.py:393
  3.4 0.0 copy-start
  3.5 0.0 copy-start.2
  3.5 30.8 %all_to_all.10 = f32[64,16,128]{2,1,0:T(8,128)S(1)} all-to-all(f32[64,16,128]{2,1,0:T(8,128)S(1)} %bitcast.11), channel_id=1, replica_groups={{0,27,54,17,44,7,34,61,24,51,14,41,4,31,58,21,48,11,38,1,28,55,18,45,8,..., dimensions={0} | all-to-all | bytes 1048576 | tf_op jit(solution)/shard_map/all_to_all | solution.py:424
  34.2 0.0 copy-done.1
  34.3 0.0 copy-done
  34.3 0.0 copy-done.2
  34.3 2.1 %shot_side.1 = (f32[2,2,32,16,128]{4,3,2,1,0:T(8,128)S(1)}, f32[8,32,128]{2,1,0:T(8,128)}) custom-call(f32[1024,128]{1,0:T(8,128)S(1)} %bitcast.10, f32[2,2,2,16,128]{4,3,2,1,0:T(8,128)S(1)} %get-tuple-element.8.corr_ref, f32[2,32,128]{2,1,0:T(8,128)S(1)} %get-tuple-element.9.window_ref, bf16[2,768,256]{2,1,0:T(8,128)(2,1)S(1)} %copy-done, ...), custom_call_target="tpu_custom_call" | custom-call | flops 1000000000 | bytes 1048576 | tf_op jit(solution)/shard_map/shot_side/pallas_call | solution.py:425
  36.4 9.1 %all-to-all-start.1 = ((f32[8,32,128]{2,1,0:T(8,128)}), f32[8,32,128]{2,1,0:T(8,128)S(1)}, u32[]{:S(2)}, u32[]{:S(2)}) async-start(f32[8,32,128]{2,1,0:T(8,128)} %get-tuple-element.11), calls=%async_computation.1 | async-start | bytes 262144 | tf_op jit(solution)/shard_map/all_to_all | solution.py:445
  45.5 1.3 %shot_side_end.1 = f32[2,32,2048]{2,1,0:T(8,128)} custom-call(f32[2,2,32,16,128]{4,3,2,1,0:T(8,128)S(1)} %get-tuple-element.10.parts_ref, f32[2,2,2,16,128]{4,3,2,1,0:T(8,128)S(1)} %get-tuple-element.8.corr_ref), custom_call_target="tpu_custom_call" | custom-call | flops 100000000 | bytes 1048576 | tf_op jit(solution)/shard_map/shot_side_end/pallas_call | solution.py:446
  46.9 6.3 %all-to-all-done.1 = f32[8,32,128]{2,1,0:T(8,128)S(1)} async-done(((f32[8,32,128]{2,1,0:T(8,128)}), f32[8,32,128]{2,1,0:T(8,128)S(1)}, u32[]{:S(2)}, u32[]{:S(2)}) %all-to-all-start.1) | async-done | bytes 131104 | tf_op jit(solution)/shard_map/all_to_all | solution.py:445
  53.2 0.6 %reduce_sum.9 = f32[32,128]{1,0:T(8,128)} reduce(f32[8,32,128]{2,1,0:T(8,128)S(1)} %all-to-all-done.1, f32[]{:T(128)} %constant.7.clone.1), dimensions={0}, to_apply=%region_0.0 | reduce | flops 28672 | bytes 147460 | tf_op jit(solution)/shard_map/reduce_sum | solution.py:455
Async XLA Ops:
  0.6 33.6 %copy-start.1 = (f32[8,2,2,32,128]{4,3,2,1,0:T(8,128)S(1)}, f32[8,2,2,32,128]{4,3,2,1,0:T(8,128)}, u32[]{:S(2)}) copy-start(f32[8,2,2,32,128]{4,3,2,1,0:T(8,128)} %constant.17.clone.e_all) | copy-start | bytes 1572868
  3.4 30.8 %copy-start = (bf16[2,768,256]{2,1,0:T(8,128)(2,1)S(1)}, bf16[2,768,256]{2,1,0:T(8,128)(2,1)}, u32[]{:S(2)}) copy-start(bf16[2,768,256]{2,1,0:T(8,128)(2,1)} %constant.21.clone.w_ref) | copy-start | bytes 2359300
  3.5 30.8 %copy-start.2 = (f32[2,2,32,128]{3,2,1,0:T(8,128)S(1)}, f32[2,2,32,128]{3,2,1,0:T(8,128)}, u32[]{:S(2)}) copy-start(f32[2,2,32,128]{3,2,1,0:T(8,128)} %constant.22.clone.tw_ref) | copy-start | bytes 196612
  36.4 16.8 %all-to-all-start.1 = ((f32[8,32,128]{2,1,0:T(8,128)}), f32[8,32,128]{2,1,0:T(8,128)S(1)}, u32[]{:S(2)}, u32[]{:S(2)}) async-start(f32[8,32,128]{2,1,0:T(8,128)} %get-tuple-element.11), calls=%async_computation.1 | async-start | bytes 262144 | tf_op jit(solution)/shard_map/all_to_all | solution.py:445
